TPU v7x, 32 devices: a whole 2x2x4 slice. The times are simulated.
32 devices in a mesh: dp: 8 (over y, x, core), seq: 4 (over z).
Axes of the slice: x: 2, y: 2, z: 4, core: 2. Of those that a mesh axis runs over, the one named last changes fastest.
Arguments:
- tokens: bfloat16 [8, 1024, 1152], P('dp', 'seq'), may hold values from -6 to 6
- timesteps: int32 [8], P('dp'), may hold values from 0 to 999
- rel_index: int32 [1024, 1024], P('seq'), may hold values from 0 to 3968, as said below
- time_table: bfloat16 [1000, 1152], replicated, may hold values from -6 to 6
- bias_table: float32 [16, 3969], replicated, may hold values from -6 to 6
- gain_one: float32 [1152], replicated, may hold values from 0.25 to 1.75
- shift_one: float32 [1152], replicated, may hold values from -4 to 4
- w_query: bfloat16 [1152, 1152], replicated, may hold values from -0.1875 to 0.1875
- w_key: bfloat16 [1152, 1152], replicated, may hold values from -0.1875 to 0.1875
- w_value: bfloat16 [1152, 1152], replicated, may hold values from -0.1875 to 0.1875
- t_query: bfloat16 [1152, 1152], replicated, may hold values from -0.1875 to 0.1875
- t_value: bfloat16 [1152, 1152], replicated, may hold values from -0.1875 to 0.1875
- b_query: float32 [1152], replicated, may hold values from -6 to 6
- b_value: float32 [1152], replicated, may hold values from -6 to 6
- w_out: bfloat16 [1152, 1152], replicated, may hold values from -1.5 to 1.5
- b_out: float32 [1152], replicated, may hold values from -4 to 4
- gain_two: float32 [1152], replicated, may hold values from 0.25 to 1.75
- shift_two: float32 [1152], replicated, may hold values from -4 to 4
- w_up: bfloat16 [1152, 4608], replicated, may hold values from -0.1875 to 0.1875
- b_up: float32 [4608], replicated, may hold values from -4 to 4
- w_down: bfloat16 [4608, 1152], replicated, may hold values from -0.09375 to 0.09375
- b_down: float32 [1152], replicated, may hold values from -4 to 4
- cotangent: bfloat16 [8, 1024, 1152], P('dp', 'seq'), may hold values from -6 to 6
Outputs:
- result: bfloat16 [8, 1024, 1152], P('dp', 'seq')
- grad_tokens: bfloat16 [8, 1024, 1152], P('dp', 'seq')
- grad_w_query: float32 [1152, 1152], P('dp', 'seq')
- grad_w_key: float32 [1152, 1152], P('dp', 'seq')
- grad_w_value: float32 [1152, 1152], P('dp', 'seq')
- grad_t_query: float32 [1152, 1152], P('dp', 'seq')
- grad_t_value: float32 [1152, 1152], P('dp', 'seq')
- grad_w_out: float32 [1152, 1152], P('dp', 'seq')
- grad_w_up: float32 [1152, 4608], P('dp', 'seq')
- grad_w_down: float32 [4608, 1152], P('dp', 'seq')
- grad_gain_one: float32 [1152], replicated
- grad_shift_one: float32 [1152], replicated
- grad_b_query: float32 [1152], replicated
- grad_b_value: float32 [1152], replicated
- grad_b_out: float32 [1152], replicated
- grad_gain_two: float32 [1152], replicated
- grad_shift_two: float32 [1152], replicated
- grad_b_up: float32 [4608], replicated
- grad_b_down: float32 [1152], replicated
- grad_bias_table: float32 [16, 3969], replicated
- grad_time_table: float32 [1000, 1152], replicated
Inputs may be any that keep to these rules, and one draw needn't show every extreme that they name: rel_index[i, j] = (r_i - r_j + 31) * 63 + c_i - c_j + 31, where token i sits at row r_i and column c_i of a 32 by 32 grid, each place taken by one token, in an order drawn from the seed.
All inputs are finite; a program needn't handle non-finite values.
Results may differ from a plain program's by a relative error of at most 0.018.
Values may be sent and summed in bfloat16 or wider, within the bound.
No kernel may reach another device: no remote copies, remote signals or barrier semaphores. Data moves between devices by JAX's collectives and lax.ppermute only.
A program may use at most 384 MiB of HBM per device.

v0:
```python
from functools import partial

import jax
import jax.numpy as jnp
from jax import lax
from jax.sharding import PartitionSpec as P

GRID = 32


norm_eps = 1e-06


def normalize(values):
    average = jnp.mean(values, axis=-1, keepdims=True)
    centered = values - average
    variance = jnp.mean(centered * centered, axis=-1, keepdims=True)
    scaled = lax.rsqrt(variance + norm_eps)
    return (centered * scaled, scaled)


def norm_back(grad_norm, normed, scaled, gain):
    inner = grad_norm * gain
    return scaled * (
        inner
        - jnp.mean(inner, axis=-1, keepdims=True)
        - normed * jnp.mean(inner * normed, axis=-1, keepdims=True)
    )


def matmul(left, right):
    return jnp.dot(left, right, preferred_element_type=jnp.float32)


def contract_rows(left, right):
    return lax.dot_general(
        left, right, (((0,), (0,)), ((), ())), preferred_element_type=jnp.float32
    )


def contract_cols(left, right):
    return lax.dot_general(
        left, right, (((1,), (1,)), ((), ())), preferred_element_type=jnp.float32
    )


def per_device(
    tokens,
    timesteps,
    rel_index,
    time_table,
    bias_table,
    gain_one,
    shift_one,
    w_query,
    w_key,
    w_value,
    t_query,
    t_value,
    b_query,
    b_value,
    w_out,
    b_out,
    gain_two,
    shift_two,
    w_up,
    b_up,
    w_down,
    b_down,
    cotangent,
):
    images, local, width = tokens.shape
    heads = bias_table.shape[0]
    head_size = width // heads
    scale = head_size ** (-0.5)
    rows = images * local
    highest = lax.Precision.HIGHEST
    table_rows = time_table.shape[0]
    grid_side = GRID
    span = 2 * grid_side - 1

    def split_heads(array):
        return array.reshape(array.shape[0], array.shape[1], heads, head_size)

    row_top = jnp.max(rel_index, axis=1)
    query_row = row_top // span - (grid_side - 1)
    query_col = row_top % span - (grid_side - 1)
    first_row = rel_index[0]
    key_row = query_row[0] - (first_row // span - (grid_side - 1))
    key_col = query_col[0] - (first_row % span - (grid_side - 1))
    key_place = key_row * grid_side + key_col
    key_order = jnp.argsort(key_place)
    offsets = jnp.arange(span, dtype=jnp.int32)
    sides = jnp.arange(grid_side, dtype=jnp.int32)
    row_mask = (
        offsets[None, None, :] == query_row[:, None, None] + grid_side - 1 - sides[None, :, None]
    ).astype(jnp.float32)
    col_mask = (
        offsets[None, None, :] == query_col[:, None, None] + grid_side - 1 - sides[None, :, None]
    ).astype(jnp.float32)
    table_square = bias_table.reshape(heads, span, span)
    bias_part = jnp.einsum("hab,icb->hiac", table_square, col_mask, precision=highest)
    bias_local = jnp.einsum("hiac,ira->hirc", bias_part, row_mask, precision=highest).reshape(
        heads, local, grid_side * grid_side
    )

    def to_grid(array):
        return jnp.take(array, key_order, axis=1)

    flat = tokens.reshape(rows, width).astype(jnp.float32)
    normed_one, scaled_one = normalize(flat)
    act_one = (normed_one * gain_one + shift_one).astype(jnp.bfloat16)
    onehot = (timesteps[:, None] == jnp.arange(table_rows, dtype=jnp.int32)[None, :]).astype(
        jnp.bfloat16
    )
    embed = matmul(onehot, time_table).astype(jnp.bfloat16)
    query_time = matmul(embed, t_query)
    value_time = matmul(embed, t_value)
    query = (
        (matmul(act_one, w_query).reshape(images, local, width) + query_time[:, None, :] + b_query)
        * scale
    ).astype(jnp.bfloat16)
    keys = matmul(act_one, w_key).reshape(images, local, width).astype(jnp.bfloat16)
    values = (
        matmul(act_one, w_value).reshape(images, local, width) + value_time[:, None, :] + b_value
    ).astype(jnp.bfloat16)
    keys_all, values_all = (
        lax.all_gather(keys, "seq", axis=1, tiled=True),
        lax.all_gather(values, "seq", axis=1, tiled=True),
    )
    keys_grid = to_grid(keys_all)
    values_grid = to_grid(values_all)
    length = keys_all.shape[1]

    def scores_of(query_img, keys_img):
        return (
            jnp.einsum("qhd,khd->hqk", query_img, keys_img, preferred_element_type=jnp.float32)
            + bias_local
        )

    def attend(inputs):
        query_img, keys_img, values_img = inputs
        scores = scores_of(query_img, keys_img)
        top = jnp.max(scores, axis=-1, keepdims=True)
        expo = jnp.exp(scores - top)
        total = jnp.sum(expo, axis=-1, keepdims=True)
        weights = (expo / total).astype(jnp.bfloat16)
        mixed_img = jnp.einsum(
            "hqk,khd->qhd", weights, values_img, preferred_element_type=jnp.float32
        )
        return (mixed_img, top[..., 0] + jnp.log(total[..., 0]))

    mixed, logsum = lax.map(
        attend, (split_heads(query), split_heads(keys_grid), split_heads(values_grid))
    )
    mixed_low = mixed.reshape(rows, width).astype(jnp.bfloat16)
    middle = flat + matmul(mixed_low, w_out) + b_out
    normed_two, scaled_two = normalize(middle)
    act_two = (normed_two * gain_two + shift_two).astype(jnp.bfloat16)
    inner = matmul(act_two, w_up) + b_up
    activated = jax.nn.gelu(inner, approximate=False).astype(jnp.bfloat16)
    result = (
        (middle + matmul(activated, w_down) + b_down)
        .astype(jnp.bfloat16)
        .reshape(images, local, width)
    )
    grad_out = cotangent.reshape(rows, width)
    grad_w_down = contract_rows(activated, grad_out)
    grad_b_down = jnp.sum(grad_out.astype(jnp.float32), axis=0)
    grad_act = contract_cols(grad_out, w_down)
    gelu_value, gelu_back = jax.vjp(partial(jax.nn.gelu, approximate=False), inner)
    grad_inner = gelu_back(grad_act)[0].astype(jnp.bfloat16)
    grad_w_up = contract_rows(act_two, grad_inner)
    grad_b_up = jnp.sum(grad_inner.astype(jnp.float32), axis=0)
    grad_norm_two = contract_cols(grad_inner, w_up)
    grad_gain_two = jnp.sum(grad_norm_two * normed_two, axis=0)
    grad_shift_two = jnp.sum(grad_norm_two, axis=0)
    grad_middle = grad_out.astype(jnp.float32) + norm_back(
        grad_norm_two, normed_two, scaled_two, gain_two
    )
    grad_branch = grad_middle.astype(jnp.bfloat16)
    grad_w_out = contract_rows(mixed_low, grad_branch)
    grad_b_out = jnp.sum(grad_branch.astype(jnp.float32), axis=0)
    grad_mixed = contract_cols(grad_branch, w_out).astype(jnp.bfloat16)
    keys_again, values_again = (
        lax.all_gather(keys, "seq", axis=1, tiled=True),
        lax.all_gather(values, "seq", axis=1, tiled=True),
    )
    keys_back, values_back = (to_grid(keys_again), to_grid(values_again))

    def attend_back(carry, inputs):
        query_img, keys_img, values_img, grad_img, logsum_img = inputs
        scores = scores_of(query_img, keys_img)
        probs = jnp.exp(scores - logsum_img[..., None])
        grad_probs = jnp.einsum(
            "qhd,khd->hqk", grad_img, values_img, preferred_element_type=jnp.float32
        )
        delta = jnp.sum(probs * grad_probs, axis=-1, keepdims=True)
        grad_scores = (probs * (grad_probs - delta)).astype(jnp.bfloat16)
        grad_query_img = jnp.einsum(
            "hqk,khd->qhd", grad_scores, keys_img, preferred_element_type=jnp.float32
        )
        grad_keys_img = jnp.einsum(
            "hqk,qhd->khd", grad_scores, query_img, preferred_element_type=jnp.float32
        )
        grad_values_img = jnp.einsum(
            "hqk,qhd->khd", probs.astype(jnp.bfloat16), grad_img, preferred_element_type=jnp.float32
        )
        return (
            carry + grad_scores.astype(jnp.float32),
            (grad_query_img.astype(jnp.bfloat16), grad_keys_img, grad_values_img),
        )

    start_carry = jnp.zeros((heads, local, length), jnp.float32)
    score_sum, (grad_query, grad_keys_grid, grad_values_grid) = lax.scan(
        attend_back,
        start_carry,
        (
            split_heads(query),
            split_heads(keys_back),
            split_heads(values_back),
            split_heads(grad_mixed.reshape(images, local, width)),
            logsum,
        ),
    )
    grad_keys_all = jnp.take(grad_keys_grid.reshape(images, length, width), key_place, axis=1)
    grad_values_all = jnp.take(grad_values_grid.reshape(images, length, width), key_place, axis=1)
    grad_keys, grad_values = (
        lax.psum_scatter(
            grad_keys_all.astype(jnp.bfloat16), "seq", scatter_dimension=1, tiled=True
        ).astype(jnp.float32),
        lax.psum_scatter(
            grad_values_all.astype(jnp.bfloat16), "seq", scatter_dimension=1, tiled=True
        ).astype(jnp.float32),
    )
    grad_keys = grad_keys.astype(jnp.bfloat16).reshape(rows, width)
    grad_values = grad_values.astype(jnp.bfloat16).reshape(rows, width)
    grad_query = grad_query.reshape(rows, width)
    grad_w_query = contract_rows(act_one, grad_query) * scale
    grad_w_key = contract_rows(act_one, grad_keys)
    grad_w_value = contract_rows(act_one, grad_values)
    query_sums = (
        jnp.sum(grad_query.astype(jnp.float32).reshape(images, local, width), axis=1) * scale
    )
    value_sums = jnp.sum(grad_values.astype(jnp.float32).reshape(images, local, width), axis=1)
    grad_b_query = jnp.sum(query_sums, axis=0)
    grad_b_value = jnp.sum(value_sums, axis=0)
    embed_wide = embed.astype(jnp.float32)
    grad_t_query = jnp.dot(embed_wide.T, query_sums, precision=highest)
    grad_t_value = jnp.dot(embed_wide.T, value_sums, precision=highest)
    grad_embed = jnp.dot(query_sums, t_query.astype(jnp.float32).T, precision=highest) + jnp.dot(
        value_sums, t_value.astype(jnp.float32).T, precision=highest
    )
    embed_rows, step_rows = (
        lax.all_gather(grad_embed, ("dp", "seq"), axis=0, tiled=True),
        lax.all_gather(timesteps, ("dp", "seq"), axis=0, tiled=True),
    )
    onehot_all = (step_rows[:, None] == jnp.arange(table_rows, dtype=jnp.int32)[None, :]).astype(
        jnp.float32
    )
    grad_time_table = jnp.dot(onehot_all.T, embed_rows, precision=highest)
    grad_norm_one = (
        scale * contract_cols(grad_query, w_query)
        + contract_cols(grad_keys, w_key)
        + contract_cols(grad_values, w_value)
    )
    grad_gain_one = jnp.sum(grad_norm_one * normed_one, axis=0)
    grad_shift_one = jnp.sum(grad_norm_one, axis=0)
    grad_tokens = (
        (grad_middle + norm_back(grad_norm_one, normed_one, scaled_one, gain_one))
        .astype(jnp.bfloat16)
        .reshape(images, local, width)
    )
    score_square = score_sum.reshape(heads, local, grid_side, grid_side)
    score_part = jnp.einsum("hirc,icb->hirb", score_square, col_mask, precision=highest)
    grad_bias_table = jnp.einsum("hirb,ira->hab", score_part, row_mask, precision=highest).reshape(
        heads, span * span
    )
    large = (
        grad_w_query,
        grad_w_key,
        grad_w_value,
        grad_t_query,
        grad_t_value,
        grad_w_out,
        grad_w_up,
        grad_w_down,
    )
    large = (
        lax.psum_scatter(large[0], "dp", scatter_dimension=0, tiled=True),
        lax.psum_scatter(large[1], "dp", scatter_dimension=0, tiled=True),
        lax.psum_scatter(large[2], "dp", scatter_dimension=0, tiled=True),
        lax.psum_scatter(large[3], "dp", scatter_dimension=0, tiled=True),
        lax.psum_scatter(large[4], "dp", scatter_dimension=0, tiled=True),
        lax.psum_scatter(large[5], "dp", scatter_dimension=0, tiled=True),
        lax.psum_scatter(large[6], "dp", scatter_dimension=0, tiled=True),
        lax.psum_scatter(large[7], "dp", scatter_dimension=0, tiled=True),
    )
    large = (
        lax.psum_scatter(
            large[0].astype(jnp.bfloat16), "seq", scatter_dimension=1, tiled=True
        ).astype(jnp.float32),
        lax.psum_scatter(
            large[1].astype(jnp.bfloat16), "seq", scatter_dimension=1, tiled=True
        ).astype(jnp.float32),
        lax.psum_scatter(
            large[2].astype(jnp.bfloat16), "seq", scatter_dimension=1, tiled=True
        ).astype(jnp.float32),
        lax.psum_scatter(
            large[3].astype(jnp.bfloat16), "seq", scatter_dimension=1, tiled=True
        ).astype(jnp.float32),
        lax.psum_scatter(
            large[4].astype(jnp.bfloat16), "seq", scatter_dimension=1, tiled=True
        ).astype(jnp.float32),
        lax.psum_scatter(
            large[5].astype(jnp.bfloat16), "seq", scatter_dimension=1, tiled=True
        ).astype(jnp.float32),
        lax.psum_scatter(
            large[6].astype(jnp.bfloat16), "seq", scatter_dimension=1, tiled=True
        ).astype(jnp.float32),
        lax.psum_scatter(
            large[7].astype(jnp.bfloat16), "seq", scatter_dimension=1, tiled=True
        ).astype(jnp.float32),
    )
    small = lax.psum(
        (
            grad_gain_one,
            grad_shift_one,
            grad_b_query,
            grad_b_value,
            grad_b_out,
            grad_gain_two,
            grad_shift_two,
            grad_b_up,
            grad_b_down,
            grad_bias_table,
        ),
        ("dp", "seq"),
    )
    return (result, grad_tokens) + tuple(large) + tuple(small) + (grad_time_table,)


def solution(mesh):
    in_specs = (
        P("dp", "seq", None),
        P("dp"),
        P("seq", None),
        P(),
        P(),
        P(),
        P(),
        P(),
        P(),
        P(),
        P(),
        P(),
        P(),
        P(),
        P(),
        P(),
        P(),
        P(),
        P(),
        P(),
        P(),
        P(),
        P("dp", "seq", None),
    )
    out_specs = (
        P("dp", "seq", None),
        P("dp", "seq", None),
        P("dp", "seq"),
        P("dp", "seq"),
        P("dp", "seq"),
        P("dp", "seq"),
        P("dp", "seq"),
        P("dp", "seq"),
        P("dp", "seq"),
        P("dp", "seq"),
        P(),
        P(),
        P(),
        P(),
        P(),
        P(),
        P(),
        P(),
        P(),
        P(),
        P(),
    )
    return jax.shard_map(
        per_device, mesh=mesh, in_specs=in_specs, out_specs=out_specs, check_vma=False
    )
```

profile of v0, /device:TPU:0, one launch (start us, length us, event | category | flops | bytes accessed | tf_op | source)
XLA Modules:
  0.0 1642.9 jit_solution(3586789408546173883)
XLA Ops:
  23.4 5.6 copy.84
  33.4 20.5 %convolution_bitcast_fusion.2 = f32[16,256,63,32]{1,2,0,3:T(8,128)} fusion(f32[16,63,63,1]{2,1,0,3:T(8,128)} %reshape.533, pred[256,32,63,1]{2,1,0,3:T(32,128)(4,1)S(1)} %fusion.17), kind=kOutput, calls=%fused_computation.15 | convolution fusion | flops 6242697216 | bytes 33800256 | tf_op jit(solution)/shard_map/hab,icb->hiac/dot_general | solution.py:102
  53.8 60.1 %copy.73 = f32[16,256,63,32]{2,3,0,1:T(8,128)} copy(f32[16,256,63,32]{1,2,0,3:T(8,128)} %convolution_bitcast_fusion.2) | data formatting | bytes 66060288 | tf_op jit(solution)/shard_map/hab,icb->hiac/transpose | solution.py:102
  114.0 158.6 %convolution_bitcast_fusion.1 = f32[16,256,32,32]{3,2,0,1:T(8,128)} fusion(pred[256,32,63,1]{2,1,3,0:T(32,128)(4,1)} %copy.84, f32[16,256,63,32]{2,3,0,1:T(8,128)} %copy.73), kind=kOutput, calls=%fused_computation.7 | convolution fusion | flops 3170893824 | bytes 50323456 | tf_op jit(solution)/shard_map/hiac,ira->hirc/dot_general | solution.py:103
  273.6 48.9 %copy.74 = f32[16,256,32,32]{1,3,2,0:T(8,128)} copy(f32[16,256,32,32]{3,2,0,1:T(8,128)} %convolution_bitcast_fusion.1) | data formatting | bytes 33554432 | tf_op jit(solution)/shard_map/hiac,ira->hirc/transpose | solution.py:103
  322.5 17.6 %copy.75 = f32[16,256,1024]{2,1,0:T(8,128)} copy(f32[16,256,1024]{1,2,0:T(8,128)} %bitcast.202) | data formatting | bytes 33554432 | tf_op jit(solution)/shard_map/reshape | solution.py:103
  354.5 8.3 gather_fusion.1
  362.8 8.3 gather_fusion
  371.1 5.1 bitcast_select_fusion.2
  384.8 14.8 fusion.94
  399.7 7.9 fusion.2
  410.3 5.3 fusion.38
  419.1 17.5 %multiply_convert_fusion.1 = (bf16[256,4608]{1,0:T(8,128)(2,1)}, f32[256,4608]{1,0:T(8,128)}, f32[256,4608]{1,0:T(8,128)}) fusion(f32[4608]{0:T(1024)S(1)} %copy-done.42, bf16[1152,4608]{1,0:T(8,128)(2,1)} %param.45, f32[256,1152]{1,0:T(8,128)S(1)} %get-tuple-element.183, f32[1152]{0:T(1024)S(1)} %copy-done.29, f32[1152]{0:T(1024)S(1)} %copy-done.26, ...), kind=kOutput, calls=%fused_computation.30 | convolution fusion | flops 2797240320 | bytes 23622656 | tf_op jit(solution)/shard_map/dot_general | solution.py:32
  436.6 14.5 convert_reduce_fusion
  451.1 8.8 multiply_reduce_fusion.1
  466.1 12.3 multiply_reduce_fusion
  478.4 9.2 fusion.4
  491.9 11.8 multiply_convert_fusion
  512.1 8.3 gather_fusion.3
  520.4 8.4 gather_fusion.2
  528.8 5.4 fusion.9
  535.3 6.9 convert_reduce_fusion.5
  546.5 4.7 fusion.81
  551.3 33.8 %reduce-scatter.35.cloned.1.call-done = bf16[1,256,1152]{2,1,0:T(8,128)(2,1)} async-done(((bf16[1,1024,1152]{2,1,0:T(8,128)(2,1)}), bf16[1,256,1152]{2,1,0:T(8,128)(2,1)}) %reduce-scatter.35.cloned.1.call-update) | async-done | bytes 589840 | tf_op jit(solution)/shard_map/reduce_scatter | solution.py:229
  585.2 4.5 fusion.60
  589.7 45.2 %reduce-scatter.37.cloned.1.call-done = bf16[1,256,1152]{2,1,0:T(8,128)(2,1)} async-done(((bf16[1,1024,1152]{2,1,0:T(8,128)(2,1)}), bf16[1,256,1152]{2,1,0:T(8,128)(2,1)}) %reduce-scatter.37.cloned.1.call-update) | async-done | bytes 589840 | tf_op jit(solution)/shard_map/reduce_scatter | solution.py:232
  634.9 4.5 fusion.57
  641.4 5.4 broadcast_multiply_fusion
  647.4 12.6 fusion.85
  660.2 13.0 fusion.63
  673.3 21.4 %reduce-scatter.39.cloned.1.call-done = f32[144,1152]{1,0:T(8,128)} async-done(((f32[1152,1152]{1,0:T(8,128)}), f32[144,1152]{1,0:T(8,128)}) %reduce-scatter.39.cloned.1.call-update) | async-done | bytes 663568 | tf_op jit(solution)/shard_map/reduce_scatter | solution.py:290
  698.6 56.6 %reduce-scatter.49.cloned.1.call-done = f32[144,1152]{1,0:T(8,128)} async-done(((f32[1152,1152]{1,0:T(8,128)}), f32[144,1152]{1,0:T(8,128)}) %reduce-scatter.49.cloned.1.call-update) | async-done | bytes 663568 | tf_op jit(solution)/shard_map/reduce_scatter | solution.py:295
  759.2 56.4 %reduce-scatter.41.cloned.1.call-done = f32[144,1152]{1,0:T(8,128)} async-done(((f32[1152,1152]{1,0:T(8,128)}), f32[144,1152]{1,0:T(8,128)}) %reduce-scatter.41.cloned.1.call-update) | async-done | bytes 663568 | tf_op jit(solution)/shard_map/reduce_scatter | solution.py:291
  819.5 56.8 %reduce-scatter.43.cloned.1.call-done = f32[144,1152]{1,0:T(8,128)} async-done(((f32[1152,1152]{1,0:T(8,128)}), f32[144,1152]{1,0:T(8,128)}) %reduce-scatter.43.cloned.1.call-update) | async-done | bytes 663568 | tf_op jit(solution)/shard_map/reduce_scatter | solution.py:292
  880.3 56.4 %reduce-scatter.45.cloned.1.call-done = f32[144,1152]{1,0:T(8,128)} async-done(((f32[1152,1152]{1,0:T(8,128)}), f32[144,1152]{1,0:T(8,128)}) %reduce-scatter.45.cloned.1.call-update) | async-done | bytes 663568 | tf_op jit(solution)/shard_map/reduce_scatter | solution.py:293
  940.6 56.6 %reduce-scatter.47.cloned.1.call-done = f32[144,1152]{1,0:T(8,128)} async-done(((f32[1152,1152]{1,0:T(8,128)}), f32[144,1152]{1,0:T(8,128)}) %reduce-scatter.47.cloned.1.call-update) | async-done | bytes 663568 | tf_op jit(solution)/shard_map/reduce_scatter | solution.py:294
  1001.4 39.3 %all-reduce = s32[32]{0:T(128)S(1)} all-reduce(s32[32]{0:T(128)S(1)} %dynamic-update-slice), channel_id=1, replica_groups=mesh['dp'=8,'seq'=4] {'dp','seq'}, use_global_device_ids=true, to_apply=%add | all-reduce | flops 32 | bytes 256
  1040.7 12.3 copy.79
  1053.0 44.2 %copy.80 = bf16[16,256,32,32]{3,2,0,1:T(8,128)(2,1)} copy(bf16[16,256,32,32]{1,3,2,0:T(8,128)(2,1)} %bitcast.203) | data formatting | bytes 16777216 | tf_op jit(solution)/shard_map/reshape | solution.py:274
  1097.2 40.9 %reduce-scatter.51.cloned.1.call-done = f32[144,4608]{1,0:T(8,128)} async-done(((f32[1152,4608]{1,0:T(8,128)}), f32[144,4608]{1,0:T(8,128)}) %reduce-scatter.51.cloned.1.call-update) | async-done | bytes 2654224 | tf_op jit(solution)/shard_map/reduce_scatter | solution.py:296
  1144.9 38.0 %convolution_bitcast_fusion = f32[16,256,32,63]{3,2,0,1:T(8,128)} fusion(bf16[16,256,32,32]{3,2,0,1:T(8,128)(2,1)} %copy.80, s32[256,32]{1,0:T(8,128)S(1)} %copy-done.18), kind=kOutput, calls=%fused_computation.6 | convolution fusion | flops 528998400 | bytes 41451520 | tf_op jit(solution)/shard_map/hirc,icb->hirb/dot_general | solution.py:275
  1182.9 95.8 %reduce-scatter.53.cloned.1.call-done = f32[576,1152]{1,0:T(8,128)} async-done(((f32[4608,1152]{1,0:T(8,128)}), f32[576,1152]{1,0:T(8,128)}) %reduce-scatter.53.cloned.1.call-update) | async-done | bytes 2654224 | tf_op jit(solution)/shard_map/reduce_scatter | solution.py:297
  1284.6 74.4 %fusion.39 = f32[16,63,63]{2,1,0:T(8,128)} fusion(f32[16,256,32,63]{3,2,0,1:T(8,128)} %convolution_bitcast_fusion, s32[256,32]{0,1:T(8,128)S(1)} %copy-done.22), kind=kOutput, calls=%fused_computation.87 | convolution fusion | flops 6243213312 | bytes 33316928 | tf_op jit(solution)/shard_map/hirb,ira->hab/dot_general | solution.py:276
  1369.3 8.2 fusion.28
  1384.9 70.1 %all-gather.3 = f32[32,1,1152]{2,1,0:T(1,128)S(1)} all-gather(f32[1,1,1152]{2,1,0:T(1,128)S(1)} %reshape.507), channel_id=4, replica_groups=mesh['dp'=8,'seq'=4] {'dp','seq'}, dimensions={0}, use_global_device_ids=true | all-gather | bytes 152064 | tf_op jit(solution)/shard_map/all_gather | solution.py:255
  1456.4 4.4 fusion.69
  1460.8 42.1 %all-reduce.1 = (f32[1152]{0:T(1024)}, f32[1152]{0:T(1024)}, f32[1152]{0:T(1024)}, f32[1152]{0:T(1024)}, f32[1152]{0:T(1024)}, /*index=5*/f32[1152]{0:T(1024)}, f32[1152]{0:T(1024)}, f32[4608]{0:T(1024)}, f32[1152]{0:T(1024)}) all-reduce(f32[1152]{0:T(1024)S(1)} %get-tuple-element.144, ...), channel_id=1, replica_groups=mesh['dp'=8,'seq'=4] {'dp','seq'}, use_global_device_ids=true, to_apply=%region_34.37 | all-reduce | flops 13824 | bytes 110592 | tf_op jit(solution)/shard_map/psum | solution.py:325
  1517.8 116.1 %all-reduce.4.cloned.1.call-done = f32[16,3969]{1,0:T(8,128)} async-done(((f32[16,3969]{1,0:T(8,128)}), f32[16,3969]{1,0:T(8,128)}) %all-reduce.4.cloned.1.call-update) | async-done | bytes 254032 | tf_op jit(solution)/shard_map/psum | solution.py:325
  (244 shorter events, 149.0 us)
Async XLA Ops:
  7.2 11.8 copy-start
  7.2 347.3 %all-gather.9.cloned.1.call-start = ((), (), s32[]{:S(2)}) async-start(), calls=%async_computation.30 | async-start | bytes 2949120 | tf_op jit(solution)/shard_map/all_gather | solution.py:128
  8.6 333.8 %copy-start.27 = (f32[256]{0:T(256)}, f32[256]{0:T(256)S(1)}, u32[]{:S(2)}) copy-start(f32[256]{0:T(256)S(1)} %broadcast_multiply_fusion.8) | copy-start | bytes 3076
  10.0 332.4 %copy-start.30 = (f32[256]{0:T(256)}, f32[256]{0:T(256)S(1)}, u32[]{:S(2)}) copy-start(f32[256]{0:T(256)S(1)} %add_rsqrt_fusion.1) | copy-start | bytes 3076
  13.9 5.2 copy-start.3
  13.9 5.2 copy-start.19
  13.9 5.2 copy-start.24
  13.9 5.2 copy-start.43
  13.9 348.9 %all-gather.7.cloned.1.call-start = ((), (), s32[]{:S(2)}) async-start(), calls=%async_computation.29 | async-start | bytes 2949120 | tf_op jit(solution)/shard_map/all_gather | solution.py:129
  20.9 8.1 copy-start.23
  21.0 564.2 %reduce-scatter.35.cloned.1.call-start = ((), (), s32[]{:S(2)}) async-start(), calls=%async_computation.18 | async-start | bytes 2949120 | tf_op jit(solution)/shard_map/reduce_scatter | solution.py:229
  399.7 10.6 copy-start.1
  410.3 5.3 copy-start.45
  418.8 41.1 %copy-start.6 = (f32[256,1152]{1,0:T(8,128)}, f32[256,1152]{1,0:T(8,128)S(1)}, u32[]{:S(2)}) copy-start(f32[256,1152]{1,0:T(8,128)S(1)} %get-tuple-element.183) | copy-start | bytes 3538948
  419.1 17.5 %copy-start.15 = (bf16[1,256,1152]{2,1,0:T(8,128)(2,1)S(1)}, bf16[1,256,1152]{2,1,0:T(8,128)(2,1)}, u32[]{:S(2)}) copy-start(bf16[1,256,1152]{2,1,0:T(8,128)(2,1)} %param.49) | copy-start | bytes 1769476
  466.1 12.3 copy-start.10
  491.9 11.8 copy-start.9
  520.4 8.4 copy-start.39
  534.2 100.7 %reduce-scatter.37.cloned.1.call-start = ((), (), s32[]{:S(2)}) async-start(), calls=%async_computation.19 | async-start | bytes 2949120 | tf_op jit(solution)/shard_map/reduce_scatter | solution.py:232
  534.8 8.2 copy-start.20
  534.8 8.2 copy-start.25
  534.8 8.2 copy-start.28
  534.8 8.2 copy-start.31
  534.8 159.8 %reduce-scatter.39.cloned.1.call-start = ((), (), s32[]{:S(2)}) async-start(), calls=%async_computation.20 | async-start | bytes 5971968 | tf_op jit(solution)/shard_map/reduce_scatter | solution.py:290
  546.5 208.7 %reduce-scatter.49.cloned.1.call-start = ((), (), s32[]{:S(2)}) async-start(), calls=%async_computation.25 | async-start | bytes 5971968 | tf_op jit(solution)/shard_map/reduce_scatter | solution.py:295
  551.3 264.3 %reduce-scatter.41.cloned.1.call-start = ((), (), s32[]{:S(2)}) async-start(), calls=%async_computation.21 | async-start | bytes 5971968 | tf_op jit(solution)/shard_map/reduce_scatter | solution.py:291
  589.7 286.6 %reduce-scatter.43.cloned.1.call-start = ((), (), s32[]{:S(2)}) async-start(), calls=%async_computation.22 | async-start | bytes 5971968 | tf_op jit(solution)/shard_map/reduce_scatter | solution.py:292
  639.4 297.2 %reduce-scatter.45.cloned.1.call-start = ((), (), s32[]{:S(2)}) async-start(), calls=%async_computation.23 | async-start | bytes 5971968 | tf_op jit(solution)/shard_map/reduce_scatter | solution.py:293
  646.8 350.5 %reduce-scatter.47.cloned.1.call-start = ((), (), s32[]{:S(2)}) async-start(), calls=%async_computation.24 | async-start | bytes 5971968 | tf_op jit(solution)/shard_map/reduce_scatter | solution.py:294
  647.4 490.7 %reduce-scatter.51.cloned.1.call-start = ((), (), s32[]{:S(2)}) async-start(), calls=%async_computation.26 | async-start | bytes 23887872 | tf_op jit(solution)/shard_map/reduce_scatter | solution.py:296
  660.0 618.8 %reduce-scatter.53.cloned.1.call-start = ((), (), s32[]{:S(2)}) async-start(), calls=%async_computation.27 | async-start | bytes 23887872 | tf_op jit(solution)/shard_map/reduce_scatter | solution.py:297
  673.2 829.7 %reduce-scatter.55.cloned.1.call-start = ((), (), s32[]{:S(2)}) async-start(), calls=%async_computation.31 | async-start | bytes 737280
  698.5 806.1 %reduce-scatter.65.cloned.1.call-start = ((), (), s32[]{:S(2)}) async-start(), calls=%async_computation.36 | async-start | bytes 737280
  759.1 747.3 %reduce-scatter.57.cloned.1.call-start = ((), (), s32[]{:S(2)}) async-start(), calls=%async_computation.32 | async-start | bytes 737280
  819.5 688.6 %reduce-scatter.59.cloned.1.call-start = ((), (), s32[]{:S(2)}) async-start(), calls=%async_computation.33 | async-start | bytes 737280
  880.2 629.6 %reduce-scatter.61.cloned.1.call-start = ((), (), s32[]{:S(2)}) async-start(), calls=%async_computation.34 | async-start | bytes 737280
  940.6 571.0 %reduce-scatter.63.cloned.1.call-start = ((), (), s32[]{:S(2)}) async-start(), calls=%async_computation.35 | async-start | bytes 737280
  1001.2 512.1 %reduce-scatter.67.cloned.1.call-start = ((), (), s32[]{:S(2)}) async-start(), calls=%async_computation.37 | async-start | bytes 2949120
  1144.9 370.7 %reduce-scatter.69.cloned.1.call-start = ((), (), s32[]{:S(2)}) async-start(), calls=%async_computation.38 | async-start | bytes 1843200
  1284.4 349.6 %all-reduce.4.cloned.1.call-start = ((), (), s32[]{:S(2)}) async-start(), calls=%async_computation.28 | async-start | bytes 524288 | tf_op jit(solution)/shard_map/psum | solution.py:325
  1365.2 4.1 copy-start.7
  1365.2 4.1 copy-start.11
  1382.3 72.8 %copy-start.5 = (f32[256,1152]{1,0:T(8,128)S(1)}, f32[256,1152]{1,0:T(8,128)}, u32[]{:S(2)}) copy-start(f32[256,1152]{1,0:T(8,128)} %copy-done.4) | copy-start | bytes 3538948
  1456.3 4.5 copy-start.34
  1456.4 4.5 copy-start.35
  1456.4 4.5 copy-start.36
  1456.4 4.5 copy-start.37
  1456.4 4.5 copy-start.38
  (20 other events, 51.1 us)
Sparse Core Ops, SparseCore 0:
  14.0 53.1 all-gather.8
  69.4 49.2 all-gather.6
  534.3 50.8 reduce-scatter.34
  587.3 47.5 reduce-scatter.36
  638.2 56.3 reduce-scatter.38
  698.3 56.8 reduce-scatter.48
  758.6 56.9 reduce-scatter.40
  819.4 56.9 reduce-scatter.42
  879.7 56.8 reduce-scatter.44
  940.3 56.9 reduce-scatter.46
  1000.9 137.1 reduce-scatter.50
  1141.5 137.1 reduce-scatter.52
  1281.6 21.9 reduce-scatter.54
  1305.8 20.2 reduce-scatter.64
  1328.8 20.2 reduce-scatter.56
  1351.2 20.3 reduce-scatter.58
  1373.8 20.3 reduce-scatter.60
  1396.3 20.6 reduce-scatter.62
  1419.3 47.1 reduce-scatter.66
  1468.6 34.3 reduce-scatter.68
  1510.1 123.8 all-reduce.3
where the time goes:
time: 1650 us; the launch traced here: 1640 us
  waiting for transfers between devices  637 us (39%)
  matrix products  474 us (29%)
  local copies, waits for them, and re-layouts  286 us (17%)
  blocking collectives  151 us (9%)
  other arithmetic  76.1 us (5%)
    dot_general x1, matrix products, per_device(): jnp.einsum('hiac,ira->hirc', bias_part, row_mask, precision=highest)  159 us
    psum x1, waiting for transfers between devices, per_device(): lax.psum((grad_gain_one, grad_shift_one, grad_b_query, grad_b_value, grad...  116 us
    reduce_scatter x1, waiting for transfers between devices, per_device(): lax.psum_scatter(large[7], 'dp', scatter_dimension=0, tiled=True)  95.8 us
    dot_general x1, matrix products, per_device(): jnp.einsum('hirb,ira->hab', score_part, row_mask, precision=highest)  74.4 us
    all_gather x1, blocking collectives, per_device(): lax.all_gather(grad_embed, ('dp', 'seq'), axis=0, tiled=True)  70.1 us
    transpose x1, local copies, waits for them, and re-layouts, per_device(): jnp.einsum('hab,icb->hiac', table_square, col_mask, precision=highest)  60.1 us
    reduce_scatter x1, waiting for transfers between devices, per_device(): lax.psum_scatter(large[2], 'dp', scatter_dimension=0, tiled=True)  56.8 us
    reduce_scatter x1, waiting for transfers between devices, per_device(): lax.psum_scatter(large[4], 'dp', scatter_dimension=0, tiled=True)  56.6 us
  transfers between devices with their start and end apart: 21, of which 11 were waited for; matrix products, arithmetic and copies ran while one was open for 40% of the time, Pallas kernels for 0%

commit v1 on v0

v1 whole, which is shorter than its diff:
```python
from functools import partial

import jax
import jax.numpy as jnp
from jax import lax
from jax.experimental import pallas as pl
from jax.experimental.pallas import tpu as pltpu
from jax.sharding import PartitionSpec as P

GRID = 32
SPAN = 2 * GRID - 1
STRIP = 2 * GRID * GRID
LANES = 128
BLOCK = 256
NORM_EPS = 1e-06
f32, bf16 = jnp.float32, jnp.bfloat16
HIGHEST = lax.Precision.HIGHEST
VMEM_LIMIT = 58 * 1024 * 1024


def dot(left, right, left_dim=1, right_dim=0):
    return lax.dot_general(
        left, right, (((left_dim,), (right_dim,)), ((), ())), preferred_element_type=f32
    )


def normalize(values):
    centered = values - jnp.mean(values, axis=-1, keepdims=True)
    scaled = lax.rsqrt(jnp.mean(centered * centered, axis=-1, keepdims=True) + NORM_EPS)
    return centered * scaled, scaled


def norm_back(grad_norm, normed, scaled, gain):
    inner = grad_norm * gain
    return scaled * (
        inner
        - jnp.mean(inner, axis=-1, keepdims=True)
        - normed * jnp.mean(inner * normed, axis=-1, keepdims=True)
    )


def fold_rows(values, op):
    return op(values.reshape(values.shape[0] // 8, 8, values.shape[1]), axis=0)


def strip_place(key_row):
    first = (GRID - 1 - key_row) * GRID
    return (first % LANES) // GRID, first // LANES * LANES


def widen(rows, height):
    fill = jnp.zeros((height - rows.shape[0], rows.shape[1]), rows.dtype)
    return jnp.concatenate([rows, fill], axis=0)


def build_permutation(place_ref, perm):
    length = perm.shape[0]

    def rows_of(i, carry):
        first = pl.multiple_of(i * BLOCK, BLOCK)
        spots = lax.broadcasted_iota(jnp.int32, (BLOCK, length), 0) + first
        hit = spots == place_ref[...]
        perm[pl.ds(first, BLOCK), :] = jnp.where(hit, 1.0, 0.0).astype(bf16)
        return carry

    lax.fori_loop(0, length // BLOCK, rows_of, 0)


def attend_kernel(
    head_size,
    x_ref,
    gain_ref,
    shift_ref,
    weight_ref,
    add_ref,
    place_ref,
    strips_ref,
    mixed_tok_ref,
    qkv_ref,
    expo_ref,
    inverse_ref,
    mixed_ref,
    hat_ref,
    perm,
    by_token,
    by_place,
    query_s,
    key_s,
    value_s,
    scores_s,
):
    head = pl.program_id(0)
    length = x_ref.shape[0]
    tiles = length // BLOCK
    group = mixed_ref.shape[0]
    scale = head_size ** (-0.5)

    @pl.when(head == 0)
    def _():
        build_permutation(place_ref, perm)

        def project(i, carry):
            span = pl.ds(pl.multiple_of(i * BLOCK, BLOCK), BLOCK)
            hat, _ = normalize(x_ref[span, :].astype(f32))
            hat_ref[span, :] = hat.astype(bf16)
            act = (hat * gain_ref[...] + shift_ref[...]).astype(bf16)
            part = dot(weight_ref[...], act, 1, 1) + add_ref[...]
            by_token[:group, span] = (part[:group] * scale).astype(bf16)
            by_token[group:, span] = part[group:].astype(bf16)
            return carry

        lax.fori_loop(0, tiles, project, 0)

        def arrange(i, carry):
            span = pl.ds(pl.multiple_of(i * BLOCK, BLOCK), BLOCK)
            part = dot(by_token[...], perm[span, :], 1, 1)
            by_place[:, span] = part
            qkv_ref[:, span] = part.astype(bf16)
            return carry

        lax.fori_loop(0, tiles, arrange, 0)

    def rows_of(which):
        first = pl.multiple_of(which * group + head * head_size, 8)
        return by_place[pl.ds(first, head_size), :]

    query_s[...] = widen(rows_of(0), LANES).astype(bf16)
    key_s[...] = jnp.transpose(widen(rows_of(1), LANES)).astype(bf16)
    value_s[...] = widen(rows_of(2), value_s.shape[0]).astype(bf16)
    own_rows = pl.ds(pl.multiple_of(head * head_size, 8), head_size)

    def tile(t, carry):
        first = pl.multiple_of(t * BLOCK, BLOCK)
        span = pl.ds(first, BLOCK)
        query = query_s[:, span]
        peak = jnp.full((8, BLOCK), -jnp.inf, f32)
        for c in range(tiles):
            keys = slice(c * BLOCK, (c + 1) * BLOCK)
            pieces = []
            for key_row in range(c * BLOCK // GRID, (c + 1) * BLOCK // GRID):
                shift, start = strip_place(key_row)
                pieces.append(strips_ref[0, shift, :, pl.ds(first + start, BLOCK)])
            scores = dot(key_s[keys, :], query) + jnp.concatenate(pieces, axis=0)
            scores_s[keys, :] = scores
            peak = jnp.maximum(peak, fold_rows(scores, jnp.max))
        peak = jnp.max(peak, axis=0, keepdims=True)
        total = jnp.zeros((8, BLOCK), f32)
        mixed = jnp.zeros((value_s.shape[0], BLOCK), f32)
        for c in range(tiles):
            keys = slice(c * BLOCK, (c + 1) * BLOCK)
            expo = jnp.exp(scores_s[keys, :] - peak)
            total = total + fold_rows(expo, jnp.sum)
            low = expo.astype(bf16)
            expo_ref[0, keys, span] = low
            mixed = mixed + dot(value_s[:, keys], low)
        inverse = 1.0 / jnp.sum(total, axis=0, keepdims=True)
        inverse_ref[0, :, span] = inverse
        mixed_ref[own_rows, span] = (mixed * inverse)[:head_size]
        return carry

    lax.fori_loop(0, tiles, tile, 0)

    @pl.when(head == pl.num_programs(0) - 1)
    def _():
        low = mixed_ref[...].astype(bf16)
        for b in range(tiles):
            mixed_tok_ref[b] = dot(low, perm[:, b * BLOCK : (b + 1) * BLOCK]).astype(bf16)


def attend_back_kernel(
    head_size,
    grad_ref,
    qkv_ref,
    expo_ref,
    inverse_ref,
    mixed_ref,
    place_ref,
    out_ref,
    strips_ref,
    perm,
    by_place,
    grad_place,
    grads,
    query_s,
    key_s,
    value_s,
    grad_s,
    grad_t,
    offset_s,
    grad_key,
    grad_value,
):
    head = pl.program_id(0)
    group, length = mixed_ref.shape
    tiles = length // BLOCK
    scale = head_size ** (-0.5)

    @pl.when(head == 0)
    def _():
        build_permutation(place_ref, perm)

        def arrange(i, carry):
            span = pl.ds(pl.multiple_of(i * BLOCK, BLOCK), BLOCK)
            part = jnp.zeros((group, BLOCK), f32)
            for b in range(tiles):
                part = part + dot(grad_ref[b], perm[span, b * BLOCK : (b + 1) * BLOCK], 1, 1)
            grad_place[:, span] = part
            by_place[:, span] = qkv_ref[:, span].astype(f32)
            return carry

        lax.fori_loop(0, tiles, arrange, 0)

    own_rows = pl.ds(pl.multiple_of(head * head_size, 8), head_size)

    def rows_of(which):
        first = pl.multiple_of(which * group + head * head_size, 8)
        return by_place[pl.ds(first, head_size), :]

    query_s[...] = jnp.transpose(widen(rows_of(0), LANES)).astype(bf16)
    key_s[...] = widen(rows_of(1), key_s.shape[0]).astype(bf16)
    value_s[...] = jnp.transpose(widen(rows_of(2), LANES)).astype(bf16)
    grad = grad_place[own_rows, :]
    inverse = inverse_ref[0]
    offset_s[...] = inverse * jnp.sum(grad * mixed_ref[own_rows, :], axis=0, keepdims=True)
    grad = widen(grad * inverse, LANES)
    grad_s[...] = grad.astype(bf16)
    grad_t[...] = jnp.transpose(grad).astype(bf16)
    grad_key[...] = jnp.zeros_like(grad_key)
    grad_value[...] = jnp.zeros_like(grad_value)
    strips_ref[...] = jnp.zeros_like(strips_ref)

    def tile(t, carry):
        first = pl.multiple_of(t * BLOCK, BLOCK)
        span = pl.ds(first, BLOCK)
        grad_tile = grad_s[:, span]
        offset = offset_s[:, span]
        grad_query = jnp.zeros((key_s.shape[0], BLOCK), f32)
        for c in range(tiles):
            keys = slice(c * BLOCK, (c + 1) * BLOCK)
            expo = expo_ref[0, keys, span]
            grad_scores = expo.astype(f32) * (dot(value_s[keys, :], grad_tile) - offset)
            for row in range(BLOCK // GRID):
                shift, start = strip_place(c * BLOCK // GRID + row)
                strips_ref[0, shift, :, pl.ds(first + start, BLOCK)] += grad_scores[
                    row * GRID : (row + 1) * GRID
                ]
            low = grad_scores.astype(bf16)
            grad_query = grad_query + dot(key_s[:, keys], low)
            grad_key[keys, :] += dot(low, query_s[span, :])
            grad_value[keys, :] += dot(expo, grad_t[span, :])
        grads[own_rows, span] = grad_query[:head_size] * scale
        return carry

    lax.fori_loop(0, tiles, tile, 0)
    for which, total in ((1, grad_key), (2, grad_value)):
        first = pl.multiple_of(which * group + head * head_size, 8)
        grads[pl.ds(first, head_size), :] = jnp.transpose(total[...])[:head_size]

    @pl.when(head == pl.num_programs(0) - 1)
    def _():
        low = grads[...].astype(bf16)
        for b in range(tiles):
            out_ref[b] = dot(low, perm[:, b * BLOCK : (b + 1) * BLOCK]).astype(bf16)


def mlp_kernel(
    mixed_ref,
    x_ref,
    dy_ref,
    w_out_ref,
    b_out_ref,
    gain_ref,
    shift_ref,
    b_down_ref,
    b_up_ref,
    w_up_ref,
    w_down_ref,
    result_ref,
    act_ref,
    inner_ref,
    norm_ref,
    middle_ref,
    branch_ref,
    grad_mixed_ref,
    sums_ref,
    up_sum_ref,
    middle_s,
    hat_s,
    scaled_s,
    result_s,
    grad_s,
):
    step = pl.program_id(0)

    @pl.when(step == 0)
    def _():
        mixed = jnp.transpose(mixed_ref[...])
        middle = x_ref[...].astype(f32) + dot(mixed, w_out_ref[...]) + b_out_ref[...]
        hat, scaled = normalize(middle)
        middle_s[...] = middle
        hat_s[...] = hat
        scaled_s[...] = scaled
        norm_ref[...] = (hat * gain_ref[...] + shift_ref[...]).astype(bf16)
        result_s[...] = jnp.zeros_like(result_s)
        grad_s[...] = jnp.zeros_like(grad_s)

    inner = dot(norm_ref[...], w_up_ref[...]) + b_up_ref[...]
    cdf = 0.5 * (1.0 + lax.erf(inner * (0.5**0.5)))
    pdf = jnp.exp(-0.5 * inner * inner) * 0.3989422804014327
    act = (inner * cdf).astype(bf16)
    grad_inner = dot(dy_ref[...], w_down_ref[...], 1, 1) * (cdf + inner * pdf)
    low = grad_inner.astype(bf16)
    act_ref[...] = jnp.transpose(act)
    inner_ref[...] = jnp.transpose(low)
    up_sum_ref[...] = jnp.sum(low.astype(f32), axis=0, keepdims=True)
    result_s[...] += dot(act, w_down_ref[...])
    grad_s[...] += dot(low, w_up_ref[...], 1, 1)

    @pl.when(step == pl.num_programs(0) - 1)
    def _():
        result_ref[...] = (middle_s[...] + result_s[...] + b_down_ref[...]).astype(bf16)
        dy = dy_ref[...].astype(f32)
        grad_norm, hat = grad_s[...], hat_s[...]
        grad_middle = dy + norm_back(grad_norm, hat, scaled_s[...], gain_ref[...])
        branch = grad_middle.astype(bf16)
        middle_ref[...] = grad_middle
        branch_ref[...] = branch
        grad_mixed_ref[...] = dot(w_out_ref[...], branch, 1, 1).astype(bf16)
        sums_ref[...] = jnp.zeros_like(sums_ref)
        sums_ref[0:1, :] = jnp.sum(dy, axis=0, keepdims=True)
        sums_ref[1:2, :] = jnp.sum(grad_norm * hat, axis=0, keepdims=True)
        sums_ref[2:3, :] = jnp.sum(grad_norm, axis=0, keepdims=True)
        sums_ref[3:4, :] = jnp.sum(branch.astype(f32), axis=0, keepdims=True)


def whole(shape):
    zeros = (0,) * len(shape)
    return pl.BlockSpec(shape, lambda s: zeros, pipeline_mode=pl.Buffered(1))


def kept(shape):
    zeros = (0,) * len(shape)
    return pl.BlockSpec(shape, lambda s: zeros)


def per_head(shape):
    rest = (0,) * (len(shape) - 1)
    return pl.BlockSpec((1,) + tuple(shape[1:]), lambda s: (s,) + rest)


def params():
    return pltpu.CompilerParams(
        dimension_semantics=("arbitrary",), vmem_limit_bytes=VMEM_LIMIT
    )


def shape_of(shape, kind):
    return jax.ShapeDtypeStruct(shape, kind)


def attend(x_all, gain, shift, weight, add, place, strips, head_size):
    length, width = x_all.shape
    heads = strips.shape[0]
    group = heads * head_size
    tall = -(-head_size // 16) * 16
    outs = (
        shape_of((length // BLOCK, group, BLOCK), bf16),
        shape_of((3 * group, length), bf16),
        shape_of((heads, length, length), bf16),
        shape_of((heads, 1, length), f32),
        shape_of((group, length), f32),
        shape_of((length, width), bf16),
    )
    return pl.pallas_call(
        partial(attend_kernel, head_size),
        grid=(heads,),
        in_specs=[whole(a.shape) for a in (x_all, gain, shift, weight, add, place)]
        + [per_head(strips.shape)],
        out_specs=[
            kept(outs[0].shape),
            kept(outs[1].shape),
            per_head(outs[2].shape),
            per_head(outs[3].shape),
            kept(outs[4].shape),
            kept(outs[5].shape),
        ],
        out_shape=outs,
        scratch_shapes=[
            pltpu.VMEM((length, length), bf16),
            pltpu.VMEM((3 * group, length), bf16),
            pltpu.VMEM((3 * group, length), f32),
            pltpu.VMEM((LANES, length), bf16),
            pltpu.VMEM((length, LANES), bf16),
            pltpu.VMEM((tall, length), bf16),
            pltpu.VMEM((length, BLOCK), f32),
        ],
        compiler_params=params(),
        name="attend",
    )(x_all, gain, shift, weight, add, place, strips)


def attend_back(grad_mixed, qkv, expo, inverse, mixed, place, head_size):
    heads, length, _ = expo.shape
    group = heads * head_size
    tall = -(-head_size // 16) * 16
    outs = (
        shape_of((length // BLOCK, 3 * group, BLOCK), bf16),
        shape_of((heads, LANES // GRID, GRID, STRIP), f32),
    )
    return pl.pallas_call(
        partial(attend_back_kernel, head_size),
        grid=(heads,),
        in_specs=[
            whole(grad_mixed.shape),
            whole(qkv.shape),
            per_head(expo.shape),
            per_head(inverse.shape),
            whole(mixed.shape),
            whole(place.shape),
        ],
        out_specs=[kept(outs[0].shape), per_head(outs[1].shape)],
        out_shape=outs,
        scratch_shapes=[
            pltpu.VMEM((length, length), bf16),
            pltpu.VMEM((3 * group, length), f32),
            pltpu.VMEM((group, length), f32),
            pltpu.VMEM((3 * group, length), f32),
            pltpu.VMEM((length, LANES), bf16),
            pltpu.VMEM((tall, length), bf16),
            pltpu.VMEM((length, LANES), bf16),
            pltpu.VMEM((LANES, length), bf16),
            pltpu.VMEM((length, LANES), bf16),
            pltpu.VMEM((1, length), f32),
            pltpu.VMEM((length, LANES), f32),
            pltpu.VMEM((length, LANES), f32),
        ],
        compiler_params=params(),
        name="attend_back",
    )(grad_mixed, qkv, expo, inverse, mixed, place)


def mlp(mixed, x, dy, w_out, b_out, gain, shift, b_down, b_up, w_up, w_down):
    rows, width = x.shape
    hidden = w_up.shape[1]
    step = 512
    outs = (
        shape_of((rows, width), bf16),
        shape_of((hidden, rows), bf16),
        shape_of((hidden, rows), bf16),
        shape_of((rows, width), bf16),
        shape_of((rows, width), f32),
        shape_of((rows, width), bf16),
        shape_of((width, rows), bf16),
        shape_of((8, width), f32),
        shape_of((1, hidden), f32),
    )
    down = pl.BlockSpec((step, rows), lambda s: (s, 0))
    return pl.pallas_call(
        mlp_kernel,
        grid=(hidden // step,),
        in_specs=[whole(a.shape) for a in (mixed, x, dy, w_out, b_out, gain, shift, b_down)]
        + [
            pl.BlockSpec((1, step), lambda s: (0, s)),
            pl.BlockSpec((width, step), lambda s: (0, s)),
            pl.BlockSpec((step, width), lambda s: (s, 0)),
        ],
        out_specs=[kept(outs[0].shape), down, down]
        + [kept(o.shape) for o in outs[3:8]]
        + [pl.BlockSpec((1, step), lambda s: (0, s))],
        out_shape=outs,
        scratch_shapes=[
            pltpu.VMEM((rows, width), f32),
            pltpu.VMEM((rows, width), f32),
            pltpu.VMEM((rows, 1), f32),
            pltpu.VMEM((rows, width), f32),
            pltpu.VMEM((rows, width), f32),
        ],
        compiler_params=params(),
        name="mlp",
    )(mixed, x, dy, w_out, b_out, gain, shift, b_down, b_up, w_up, w_down)


def key_places(rel_index):
    first = rel_index[0]
    top = jnp.max(first)
    row = top // SPAN - first // SPAN
    column = top % SPAN - first % SPAN
    return (row * GRID + column)[None, :].astype(jnp.int32)


def bias_strips(table):
    heads = table.shape[0]
    square = table.reshape(heads, SPAN, SPAN)
    strip = jnp.stack(
        [square[:, :, GRID - 1 - c : SPAN - c] for c in range(GRID)], axis=1
    ).reshape(heads, GRID, SPAN * GRID)
    strip = jnp.pad(strip, ((0, 0), (0, 0), (0, STRIP + LANES - SPAN * GRID)))
    return jnp.stack(
        [strip[:, :, s * GRID : s * GRID + STRIP] for s in range(LANES // GRID)], axis=1
    )


def table_grad(strips):
    heads = strips.shape[0]
    total = sum(
        jnp.pad(strips[:, s], ((0, 0), (0, 0), (s * GRID, LANES - s * GRID)))
        for s in range(LANES // GRID)
    )
    parts = total[:, :, : SPAN * GRID].reshape(heads, GRID, SPAN, GRID)
    sides = jnp.arange(GRID, dtype=jnp.int32)
    place = GRID - 1 - sides[:, None] + sides[None, :]
    onehot = (place[:, :, None] == jnp.arange(SPAN, dtype=jnp.int32)).astype(f32)
    return jnp.einsum("hjai,jib->hab", parts, onehot, precision=HIGHEST).reshape(
        heads, SPAN * SPAN
    )


def per_device(
    tokens,
    timesteps,
    rel_index,
    time_table,
    bias_table,
    gain_one,
    shift_one,
    w_query,
    w_key,
    w_value,
    t_query,
    t_value,
    b_query,
    b_value,
    w_out,
    b_out,
    gain_two,
    shift_two,
    w_up,
    b_up,
    w_down,
    b_down,
    cotangent,
):
    _, local, width = tokens.shape
    hidden = w_up.shape[1]
    heads = bias_table.shape[0]
    head_size = width // heads
    n_dp, n_seq = lax.axis_size("dp"), lax.axis_size("seq")
    dp, seq = lax.axis_index("dp"), lax.axis_index("seq")
    own_heads = heads // n_seq
    group = own_heads * head_size
    scale = head_size ** (-0.5)
    table_rows = time_table.shape[0]

    def own_columns(array):
        return lax.dynamic_slice_in_dim(array, seq * group, group, axis=array.ndim - 1)

    x = tokens[0]
    dy = cotangent[0]
    x_all = lax.all_gather(x, "seq", axis=0, tiled=True)
    dy_all = lax.all_gather(dy, "dp", axis=0)
    steps_all = lax.all_gather(timesteps, "dp", axis=0, tiled=True)

    place = key_places(rel_index)
    strips = bias_strips(lax.dynamic_slice_in_dim(bias_table, seq * own_heads, own_heads, 0))
    weight = jnp.concatenate([own_columns(w).T for w in (w_query, w_key, w_value)], axis=0)
    embed = lax.dynamic_slice_in_dim(time_table, timesteps[0], 1, 0)
    tq_own, tv_own = own_columns(t_query), own_columns(t_value)
    query_add = dot(embed, tq_own)[0] + own_columns(b_query)
    value_add = dot(embed, tv_own)[0] + own_columns(b_value)
    add = jnp.concatenate([query_add, jnp.zeros((group,), f32), value_add])[:, None]

    mixed_tok, qkv, expo, inverse, mixed, hat_one = attend(
        x_all, gain_one[None], shift_one[None], weight, add, place, strips, head_size
    )
    mixed_own = lax.all_to_all(mixed_tok, "seq", 0, 0).reshape(width, local)
    (
        result,
        act_t,
        inner_t,
        norm_two,
        grad_middle,
        branch,
        grad_mixed,
        sums_two,
        up_sum,
    ) = mlp(
        mixed_own,
        x,
        dy,
        w_out,
        b_out[None],
        gain_two[None],
        shift_two[None],
        b_down[None],
        b_up[None],
        w_up,
        w_down,
    )
    norm_all = lax.all_gather(norm_two, "dp", axis=0)
    branch_all = lax.all_gather(branch, "dp", axis=0)
    grad_heads = lax.all_to_all(grad_mixed.reshape(n_seq, group, local), "seq", 0, 0)

    down_rows, out_rows = hidden // n_dp, width // n_dp
    up_columns = hidden // n_dp // n_seq
    parts = jnp.concatenate(
        [
            act_t.reshape(n_dp, down_rows, local),
            jnp.swapaxes(inner_t.reshape(n_seq, n_dp, up_columns, local), 0, 1).reshape(
                n_dp, down_rows, local
            ),
            mixed_own.reshape(n_dp, out_rows, local),
        ],
        axis=1,
    )
    parts = lax.all_to_all(parts, "dp", 0, 0)

    def over_sources(left, right):
        return lax.dot_general(
            left, right, (((0, 2), (0, 1)), ((), ())), preferred_element_type=f32
        )

    part_down = over_sources(parts[:, :down_rows], dy_all)
    part_up = over_sources(parts[:, down_rows : 2 * down_rows], norm_all)
    part_out = over_sources(parts[:, 2 * down_rows :], branch_all)
    by_column = lax.psum_scatter(
        jnp.concatenate([part_down, part_out], axis=0).astype(bf16),
        "seq",
        scatter_dimension=1,
        tiled=True,
    ).astype(f32)
    grad_w_down, grad_w_out = by_column[:down_rows], by_column[down_rows:]
    up_t = lax.psum_scatter(
        part_up.astype(bf16).reshape(n_seq, up_columns, width), "seq", scatter_dimension=0
    )
    up_t = lax.all_to_all(
        up_t.reshape(up_columns, n_dp, out_rows), "dp", split_axis=1, concat_axis=0
    )
    grad_w_up = jnp.transpose(up_t.reshape(hidden // n_seq, out_rows)).astype(f32)

    grads, grad_strips = attend_back(
        grad_heads, qkv, expo, inverse, mixed, place, head_size
    )
    grads_all = lax.all_to_all(grads, "seq", 0, 0)
    product = lax.dot_general(
        hat_one.reshape(n_seq, local, width),
        grads,
        (((0, 1), (0, 2)), ((), ())),
        preferred_element_type=f32,
    )
    grad_sums = jnp.sum(grads.astype(f32), axis=(0, 2))
    weight_wide = weight.T.astype(f32)
    grad_gain_one = jnp.sum(product * weight_wide, axis=1)
    grad_shift_one = jnp.sum(weight_wide * grad_sums[None, :], axis=1)
    grad_qkv = gain_one[:, None] * product + shift_one[:, None] * grad_sums[None, :]
    grad_qkv = lax.psum_scatter(
        grad_qkv.astype(bf16), "dp", scatter_dimension=0, tiled=True
    ).astype(f32)

    pieces = grads_all.reshape(n_seq, 3, group, local)
    grad_norm_one = sum(
        lax.dot_general(
            pieces[:, which].reshape(width, local),
            w,
            (((0,), (1,)), ((), ())),
            preferred_element_type=f32,
        )
        for which, w in enumerate((w_query, w_key, w_value))
    )
    hat_local, scaled_local = normalize(x.astype(f32))
    grad_tokens = (
        grad_middle + norm_back(grad_norm_one, hat_local, scaled_local, gain_one)
    ).astype(bf16)

    query_sum, value_sum = grad_sums[:group], grad_sums[2 * group :]
    grad_embed = jnp.dot(tq_own.astype(f32), query_sum, precision=HIGHEST) + jnp.dot(
        tv_own.astype(f32), value_sum, precision=HIGHEST
    )
    own_image = lax.broadcasted_iota(jnp.int32, (n_dp, 1), 0) == dp

    def slot(row):
        return jnp.where(own_image, row[None, :], 0.0).reshape(-1)

    apart = [table_grad(grad_strips).reshape(-1), query_sum, value_sum]
    summed = [
        slot(grad_embed),
        up_sum[0],
        sums_two[:4].reshape(-1),
        grad_gain_one,
        grad_shift_one,
    ]
    images = [slot(jnp.concatenate([query_sum, value_sum]))]
    sizes = [sum(a.shape[0] for a in part) for part in (apart, summed, images)]
    vector = lax.psum(jnp.concatenate(apart + summed + images), "dp")
    image_sums = vector[sizes[0] + sizes[1] :].reshape(n_dp, 2 * group)
    vector = lax.all_gather(vector[: sizes[0] + sizes[1]], "seq", axis=0)
    table_size = own_heads * SPAN * SPAN
    grad_bias_table = vector[:, :table_size].reshape(heads, SPAN * SPAN)
    grad_b_query = vector[:, table_size : table_size + group].reshape(-1)
    grad_b_value = vector[:, table_size + group : sizes[0]].reshape(-1)
    both = jnp.sum(vector[:, sizes[0] :], axis=0)
    embed_size = n_dp * width
    embed_rows = both[:embed_size].reshape(n_dp, width)
    grad_b_up = both[embed_size : embed_size + hidden]
    rest = both[embed_size + hidden :].reshape(6, width)
    grad_b_down, grad_gain_two, grad_shift_two, grad_b_out, grad_gain_one, grad_shift_one = (
        rest[r] for r in range(6)
    )

    embeds = lax.dynamic_slice_in_dim(
        jnp.take(time_table, steps_all, axis=0), dp * out_rows, out_rows, axis=1
    ).astype(f32)
    grad_t_query = jnp.dot(embeds.T, image_sums[:, :group], precision=HIGHEST)
    grad_t_value = jnp.dot(embeds.T, image_sums[:, group:], precision=HIGHEST)
    onehot = (
        steps_all[:, None] == jnp.arange(table_rows, dtype=jnp.int32)[None, :]
    ).astype(f32)
    grad_time_table = jnp.dot(onehot.T, embed_rows, precision=HIGHEST)

    return (
        result[None],
        grad_tokens[None],
        grad_qkv[:, :group],
        grad_qkv[:, group : 2 * group],
        grad_qkv[:, 2 * group :],
        grad_t_query,
        grad_t_value,
        grad_w_out,
        grad_w_up,
        grad_w_down,
        grad_gain_one,
        grad_shift_one,
        grad_b_query,
        grad_b_value,
        grad_b_out,
        grad_gain_two,
        grad_shift_two,
        grad_b_up,
        grad_b_down,
        grad_bias_table,
        grad_time_table,
    )


def solution(mesh):
    split, copied, by_block = P("dp", "seq", None), P(), P("dp", "seq")
    in_specs = (split, P("dp"), P("seq", None)) + (copied,) * 19 + (split,)
    out_specs = (split, split) + (by_block,) * 8 + (copied,) * 11
    return jax.shard_map(
        per_device, mesh=mesh, in_specs=in_specs, out_specs=out_specs, check_vma=False
    )
```

time: 1650 us -> 648 us (0.39)
  matrix products: 474 us -> 47.5 us
  waiting for transfers between devices: 637 us -> 229 us
  local copies, waits for them, and re-layouts: 286 us -> 134 us
  Pallas kernels: 0 us -> 80.4 us
  blocking collectives: 151 us -> 88.9 us
  other arithmetic: 76.1 us -> 21.9 us
  starting transfers between devices: 1.66 us -> 18.6 us
    reduce_scatter x10 -> x1, waiting for transfers between devices: 520 us -> 7.01 us  [per_device(): lax.psum_scatter(part_up.astype(bf16).reshape(n_seq, up_columns, width),...]
    dot_general x34 -> x15, matrix products: 474 us -> 47.5 us  [the longest x3 18.3 us: over_sources(): lax.dot_general(left, right, (((0, 2), (0, 1)), ((), ())), preferred_elem...]
    transpose x2 -> x1, local copies, waits for them, and re-layouts: 109 us -> 1.85 us  [per_device(): jnp.swapaxes(inner_t.reshape(n_seq, n_dp, up_columns, local), 0, 1)]
    all_to_all x0 -> x1, blocking collectives: none -> 82.3 us  [per_device(): parts = lax.all_to_all(parts, 'dp', 0, 0)]
    pallas_call x0 -> x3, Pallas kernels: none -> 80.4 us  [the longest x1 29.1 us: attend(): pl.pallas_call(partial(attend_kernel, head_size), grid=(heads,), in_specs...]
    unnamed x29 -> x12, waiting for transfers between devices: 1.38 us -> 79.3 us
    all_gather x1 -> x0, blocking collectives: 70.1 us -> none  [per_device(): lax.all_gather(grad_embed, ('dp', 'seq'), axis=0, tiled=True)]
    all_gather x2 -> x4, waiting for transfers between devices: 0.02 us -> 67.7 us  [the longest x1 34.3 us: per_device(): dy_all = lax.all_gather(dy, 'dp', axis=0)]
  transfers between devices with their start and end apart: 21 -> 13, of which waited for: 11 -> 9; matrix products, arithmetic and copies ran while one was open for 40% -> 26% of each run, Pallas kernels for 0% -> 0%
where the time goes in v1:
time: 648 us; the launch traced here: 638 us
  waiting for transfers between devices  229 us (35%)
  local copies, waits for them, and re-layouts  134 us (21%)
  blocking collectives  88.9 us (14%)
  Pallas kernels  80.4 us (12%)
  matrix products  47.5 us (7%)
  other arithmetic  21.9 us (3%)
  starting transfers between devices  18.6 us (3%)
  between operations  17.9 us (3%)
    all_to_all x1, blocking collectives, per_device(): parts = lax.all_to_all(parts, 'dp', 0, 0)  82.3 us
    unnamed x12, waiting for transfers between devices  79.3 us
    another operation x33, local copies, waits for them, and re-layouts, bias_strips(): jnp.stack([square[:, :, GRID - 1 - c:SPAN - c] for c in range(GRID)], axi...  52.6 us
    psum x1, waiting for transfers between devices, per_device(): vector = lax.psum(jnp.concatenate(apart + summed + images), 'dp')  48.9 us
    all_gather x1, waiting for transfers between devices, per_device(): dy_all = lax.all_gather(dy, 'dp', axis=0)  34.3 us
    all_gather x1, waiting for transfers between devices, per_device(): branch_all = lax.all_gather(branch, 'dp', axis=0)  33.4 us
    unnamed x78, local copies, waits for them, and re-layouts  30.5 us
    pallas_call x1, Pallas kernels, attend(): pl.pallas_call(partial(attend_kernel, head_size), grid=(heads,), in_specs...  29.1 us
  transfers between devices with their start and end apart: 13, of which 9 were waited for; matrix products, arithmetic and copies ran while one was open for 26% of the time, Pallas kernels for 0%

profile of v1, /device:TPU:0, one launch (start us, length us, event | category | flops | bytes accessed | tf_op | source)
XLA Modules:
  0.0 638.4 jit_solution(15452672490137371530)
XLA Ops:
  14.0 3.5 constant_dynamic-slice_fusion.1
  17.4 2.3 copy.216
  45.7 2.0 fusion.51
  77.9 7.7 %stack.146 = f32[4,32,2016]{2,1,0:T(8,128)} concatenate(f32[4,1,2016]{2,1,0:T(1,128)S(1)} %stack.152, f32[4,1,2016]{2,1,0:T(1,128)S(1)} %stack.153, f32[4,1,2016]{2,1,0:T(1,128)S(1)} %stack.154, f32[4,1,2016]{2,1,0:T(1,128)} %stack.155, f32[4,1,2016]{2,1,0:T(1,128)} %stack.156, f32[4,1,2016]{2,1,0:T(1,128)} %stack.157, f32[4,1,2016]{2,1,0:T(1,128)} %stack.158, ...), dimensions={1} | concatenate | bytes 2064384 | tf_op jit(solution)/shard_map/stack | solution.py:494
  87.0 2.7 pad_maximum_fusion.2.weight_ref
  90.6 2.3 pad_maximum_fusion.1.strips_ref
  93.0 29.1 %attend.1 = (bf16[4,288,256]{2,1,0:T(8,128)(2,1)}, bf16[864,1024]{1,0:T(8,128)(2,1)}, bf16[4,1024,1024]{2,1,0:T(8,128)(2,1)}, f32[4,1,1024]{2,1,0:T(1,128)}, f32...) custom-call(bf16[1024,1152]{1,0:T(8,128)(2,1)} %bitcast.142, f32[1,1152]{1,0:T(1,128)} %broadcast_in_dim.103.gain_ref, ...), custom_call_target="tpu_custom_call" | custom-call | tf_op jit(solution)/shard_map/attend/pallas_call | solution.py:374
  122.1 6.0 all-to-all-start
  131.1 12.9 %all-to-all-done = bf16[4,288,256]{2,1,0:T(8,128)(2,1)S(1)} async-done(((bf16[4,288,256]{2,1,0:T(8,128)(2,1)}), bf16[4,288,256]{2,1,0:T(8,128)(2,1)S(1)}, u32[]{:S(2)}, u32[]{:S(2)}) %all-to-all-start) | async-done | bytes 589856 | tf_op jit(solution)/shard_map/all_to_all | solution.py:575
  144.8 23.9 %mlp.1 = (bf16[256,1152]{1,0:T(8,128)(2,1)}, bf16[4608,256]{1,0:T(8,128)(2,1)}, bf16[4608,256]{1,0:T(8,128)(2,1)}, bf16[256,1152]{1,0:T(8,128)(2,1)}, f32[256,11...) custom-call(bf16[1152,256]{1,0:T(8,128)(2,1)} %bitcast.126, ...), custom_call_target="tpu_custom_call" | custom-call | tf_op jit(solution)/shard_map/mlp/pallas_call | solution.py:458
  168.8 3.5 all-to-all-start.1
  174.0 13.7 %all-to-all-done.1.grad_ref = bf16[4,288,256]{2,1,0:T(8,128)(2,1)S(1)} async-done(((bf16[4,288,256]{2,1,0:T(8,128)(2,1)}), bf16[4,288,256]{2,1,0:T(8,128)(2,1)S(1)}, u32[]{:S(2)}, u32[]{:S(2)}) %all-to-all-start.1) | async-done | bytes 589856 | tf_op jit(solution)/shard_map/all_to_all | solution.py:601
  188.5 27.4 %attend_back.1 = (bf16[4,864,256]{2,1,0:T(8,128)(2,1)}, f32[4,4,32,2048]{3,2,1,0:T(8,128)}) custom-call(bf16[4,288,256]{2,1,0:T(8,128)(2,1)} %copy-done.13, bf16[864,1024]{1,0:T(8,128)(2,1)} %get-tuple-element.42.qkv_ref, bf16[4,1024,1024]{2,1,0:T(8,128)(2,1)} %get-tuple-element.43.expo_ref, f32[4,1,1024]{2,1,0:T(1,128)} %get-tuple-element.44.inverse_ref, ...), custom_call_target="tpu_custom_call" | custom-call | tf_op jit(solution)/shard_map/attend_back/pallas_call | solution.py:410
  217.2 2.4 slice_bitcast_fusion.2
  220.9 5.6 fusion.1
  226.6 1.9 pad_add_fusion
  228.4 3.9 reshape.265
  232.3 4.1 convolution_bitcast_fusion.3
  236.7 2.2 convolution_reduce_fusion.1
  238.9 2.2 convolution_reduce_fusion
  244.2 48.9 %all-reduce.10.cloned.1.call-done = f32[41796]{0:T(1024)} async-done(((f32[41796]{0:T(1024)}), f32[41796]{0:T(1024)}) %all-reduce.10.cloned.1.call-update) | async-done | bytes 167200 | tf_op jit(solution)/shard_map/psum | solution.py:693
  296.7 1.9 copy.201
  298.6 2.0 pad_maximum_fusion
  300.6 82.3 %all_to_all.29 = bf16[8,1296,256]{2,1,0:T(8,128)(2,1)} all-to-all(bf16[8,1296,256]{2,1,0:T(8,128)(2,1)S(1)} %pad_maximum_fusion), channel_id=1, replica_groups=mesh['dp'=8,'seq'=4] {'dp'}, dimensions={0} | all-to-all | bytes 10616832 | tf_op jit(solution)/shard_map/all_to_all | solution.py:615
  382.9 7.4 %fusion.5 = bf16[576,1152]{1,0:T(8,128)(2,1)} fusion(bf16[8,256,1152]{2,1,0:T(8,128)(2,1)} %bitcast.148, bf16[8,1296,256]{2,1,0:T(8,128)(2,1)} %all_to_all.29), kind=kOutput, calls=%fused_computation.14 | convolution fusion | flops 2718572544 | bytes 8404992 | tf_op jit(solution)/shard_map/dot_general | solution.py:618
  391.8 6.5 %all-reduce.5 = s32[8]{0:T(128)S(1)} all-reduce(s32[8]{0:T(128)S(1)} %dynamic-update-slice), channel_id=1, replica_groups=mesh['dp'=8,'seq'=4] {'dp'}, use_global_device_ids=true, to_apply=%add.5 | all-reduce | flops 8 | bytes 64
  398.3 2.5 gather_fusion
  401.0 4.1 copy.210
  406.1 4.6 all-to-all-start.2
  413.7 14.0 %all-reduce.12.cloned.1.call-done = f32[148752]{0:T(1024)} async-done(((f32[148752]{0:T(1024)}), f32[148752]{0:T(1024)}) %all-reduce.12.cloned.1.call-update) | async-done | bytes 595024
  427.6 2.3 reshape.288
  432.4 34.3 %all-gather.9.cloned.1.call-done = bf16[8,256,1152]{2,1,0:T(8,128)(2,1)} async-done(((bf16[1,256,1152]{2,1,0:T(8,128)(2,1)}), bf16[8,256,1152]{2,1,0:T(8,128)(2,1)}) %all-gather.9.cloned.1.call-update) | async-done | bytes 4718608 | tf_op jit(solution)/shard_map/all_gather | solution.py:560
  466.8 7.3 %fusion.4 = bf16[576,1152]{1,0:T(8,128)(2,1)} fusion(bf16[8,256,1152]{2,1,0:T(8,128)(2,1)} %all-gather.9.cloned.1.call-done, bf16[8,1296,256]{2,1,0:T(8,128)(2,1)} %all_to_all.29), kind=kOutput, calls=%fused_computation.13 | convolution fusion | flops 2718572544 | bytes 8404992 | tf_op jit(solution)/shard_map/dot_general | solution.py:618
  474.1 33.4 %all-gather.13.cloned.1.call-done = bf16[2048,1152]{1,0:T(8,128)(2,1)} async-done(((bf16[256,1152]{1,0:T(8,128)(2,1)}), bf16[2048,1152]{1,0:T(8,128)(2,1)}) %all-gather.13.cloned.1.call-update) | async-done | bytes 4718608 | tf_op jit(solution)/shard_map/all_gather | solution.py:600
  507.4 3.6 fusion.7
  512.3 4.0 copy.212
  522.1 5.1 fusion.29
  532.2 2.2 fusion.47
  534.4 7.0 %reduce-scatter.8.cloned.1.call-done = bf16[1,144,1152]{2,1,0:T(8,128)(2,1)} async-done(((bf16[4,144,1152]{2,1,0:T(8,128)(2,1)}), bf16[1,144,1152]{2,1,0:T(8,128)(2,1)}) %reduce-scatter.8.cloned.1.call-update) | async-done | bytes 331792 | tf_op jit(solution)/shard_map/reduce_scatter | solution.py:632
  541.4 2.0 copy.202
  543.5 4.2 all-to-all-start.4
  547.7 3.0 fusion.24
  550.7 33.8 %reduce-scatter.10.cloned.1.call-done = bf16[144,864]{1,0:T(8,128)(2,1)} async-done(((bf16[1152,864]{1,0:T(8,128)(2,1)}), bf16[144,864]{1,0:T(8,128)(2,1)}) %reduce-scatter.10.cloned.1.call-update) | async-done | bytes 248848
  586.5 1.8 copy.204
  588.3 1.8 copy.205
  593.8 2.5 reshape.275
  596.3 29.0 %reduce-scatter.12.cloned.1.call-done = bf16[288,720]{1,0:T(8,128)(2,1)} async-done(((bf16[1152,720]{1,0:T(8,128)(2,1)}), bf16[288,720]{1,0:T(8,128)(2,1)}) %reduce-scatter.12.cloned.1.call-update) | async-done | bytes 414736
  626.3 1.9 slice.362
  (199 shorter events, 107.9 us)
Async XLA Ops:
  7.2 13.7 %copy-start = (bf16[1152,1152]{1,0:T(8,128)(2,1)S(1)}, bf16[1152,1152]{1,0:T(8,128)(2,1)}, u32[]{:S(2)}) copy-start(bf16[1152,1152]{1,0:T(8,128)(2,1)} %param.30) | copy-start | bytes 7962628
  7.2 85.7 %all-gather.11.cloned.1.call-start = ((), (), s32[]{:S(2)}) async-start(), calls=%async_computation.11 | async-start | bytes 2949120 | tf_op jit(solution)/shard_map/all_gather | solution.py:559
  47.7 39.3 %copy-start.8 = (bf16[1152,288]{0,1:T(8,128)(2,1)S(1)}, bf16[1152,288]{0,1:T(8,128)(2,1)}, u32[]{:S(2)}) copy-start(bf16[1152,288]{0,1:T(8,128)(2,1)} %copy.216) | copy-start | bytes 1990660
  85.5 4.2 copy-start.7
  92.9 35.2 %copy-start.21 = (f32[1152]{0:T(1024)S(1)}, f32[1152]{0:T(1024)}, u32[]{:S(2)}) copy-start(f32[1152]{0:T(1024)} %param.38) | copy-start | bytes 13828
  92.9 35.8 %copy-start.22 = (f32[1152]{0:T(1024)S(1)}, f32[1152]{0:T(1024)}, u32[]{:S(2)}) copy-start(f32[1152]{0:T(1024)} %param.39) | copy-start | bytes 13828
  92.9 36.4 %copy-start.23 = (f32[1152]{0:T(1024)S(1)}, f32[1152]{0:T(1024)}, u32[]{:S(2)}) copy-start(f32[1152]{0:T(1024)} %param.40) | copy-start | bytes 13828
  92.9 37.0 %copy-start.24 = (f32[1152]{0:T(1024)S(1)}, f32[1152]{0:T(1024)}, u32[]{:S(2)}) copy-start(f32[1152]{0:T(1024)} %param.44) | copy-start | bytes 13828
  92.9 37.6 %copy-start.17 = (f32[4608]{0:T(1024)S(1)}, f32[4608]{0:T(1024)}, u32[]{:S(2)}) copy-start(f32[4608]{0:T(1024)} %param.42) | copy-start | bytes 55300
  122.1 21.9 %all-to-all-start = ((bf16[4,288,256]{2,1,0:T(8,128)(2,1)}), bf16[4,288,256]{2,1,0:T(8,128)(2,1)S(1)}, u32[]{:S(2)}, u32[]{:S(2)}) async-start(bf16[4,288,256]{2,1,0:T(8,128)(2,1)} %get-tuple-element.38), calls=%async_computation | async-start | bytes 1179648 | tf_op jit(solution)/shard_map/all_to_all | solution.py:575
  144.0 0.8 copy-start.3
  168.8 18.9 %all-to-all-start.1 = ((bf16[4,288,256]{2,1,0:T(8,128)(2,1)}), bf16[4,288,256]{2,1,0:T(8,128)(2,1)S(1)}, u32[]{:S(2)}, u32[]{:S(2)}) async-start(bf16[4,288,256]{2,1,0:T(8,128)(2,1)} %bitcast.147), calls=%async_computation.1 | async-start | bytes 1179648 | tf_op jit(solution)/shard_map/all_to_all | solution.py:601
  172.3 120.9 %all-reduce.10.cloned.1.call-start = ((), (), s32[]{:S(2)}) async-start(), calls=%async_computation.8 | async-start | bytes 335872 | tf_op jit(solution)/shard_map/psum | solution.py:693
  187.6 0.9 copy-start.13
  217.1 2.4 copy-start.2
  217.2 2.9 copy-start.9
  217.2 2.9 copy-start.10
  217.2 2.9 copy-start.11
  217.2 2.9 copy-start.16
  217.2 2.9 copy-start.25
  217.2 3.7 copy-start.27
  236.5 6.5 %copy-start.29 = (u32[32]{0:T(128)S(1)}, u32[32]{0:T(128)}, u32[]{:S(2)}) copy-start(u32[32]{0:T(128)} %constant.103) | copy-start | bytes 388
  242.2 140.8 %all-gather.15.cloned.1.call-start = ((), (), s32[]{:S(2)}) async-start(), calls=%async_computation.13 | async-start | bytes 5308416 | tf_op jit(solution)/shard_map/all_gather | solution.py:599
  242.9 184.7 %all-reduce.12.cloned.1.call-start = ((), (), s32[]{:S(2)}) async-start(), calls=%async_computation.14 | async-start | bytes 1196032
  294.7 0.8 copy-start.12
  295.5 171.2 %all-gather.9.cloned.1.call-start = ((), (), s32[]{:S(2)}) async-start(), calls=%async_computation.9 | async-start | bytes 5308416 | tf_op jit(solution)/shard_map/all_gather | solution.py:560
  296.1 211.3 %all-gather.13.cloned.1.call-start = ((), (), s32[]{:S(2)}) async-start(), calls=%async_computation.12 | async-start | bytes 5308416 | tf_op jit(solution)/shard_map/all_gather | solution.py:600
  296.2 2.4 copy-start.4
  296.7 244.7 %reduce-scatter.8.cloned.1.call-start = ((), (), s32[]{:S(2)}) async-start(), calls=%async_computation.10 | async-start | bytes 1658880 | tf_op jit(solution)/shard_map/reduce_scatter | solution.py:632
  382.9 7.5 %copy-start.28 = (u32[32]{0:T(128)S(1)}, u32[32]{0:T(128)}, u32[]{:S(2)}) copy-start(u32[32]{0:T(128)} %constant.98) | copy-start | bytes 388
  382.9 17.9 %copy-start.1 = (bf16[1,256,1152]{2,1,0:T(8,128)(2,1)S(1)}, bf16[1,256,1152]{2,1,0:T(8,128)(2,1)}, u32[]{:S(2)}) copy-start(bf16[1,256,1152]{2,1,0:T(8,128)(2,1)} %param.23) | copy-start | bytes 1769476
  390.4 194.1 %reduce-scatter.10.cloned.1.call-start = ((), (), s32[]{:S(2)}) async-start(), calls=%async_computation.15 | async-start | bytes 2322432
  398.3 7.2 %copy-start.26 = (s32[8]{0:T(128)}, s32[8]{0:T(128)S(1)}, u32[]{:S(2)}) copy-start(s32[8]{0:T(128)S(1)} %all-reduce.5) | copy-start | bytes 100
  405.2 5.5 copy-start.18
  406.1 121.1 %all-to-all-start.2 = ((bf16[4,864,256]{2,1,0:T(8,128)(2,1)}), bf16[4,864,256]{2,1,0:T(8,128)(2,1)}, u32[]{:S(2)}, u32[]{:S(2)}) async-start(bf16[4,864,256]{2,1,0:T(8,128)(2,1)} %get-tuple-element.46), calls=%async_computation.2 | async-start | bytes 3538944 | tf_op jit(solution)/shard_map/all_to_all | solution.py:643
  410.7 214.6 %reduce-scatter.12.cloned.1.call-start = ((), (), s32[]{:S(2)}) async-start(), calls=%async_computation.16 | async-start | bytes 2211840
  431.2 0.6 copy-start.15
  507.4 3.6 copy-start.14
  512.3 8.9 %slice-start = ((f32[4,37188]{1,0:T(4,128)}), f32[4,15876]{1,0:T(4,128)S(1)}, s32[]{:S(2)}) async-start(f32[4,37188]{1,0:T(4,128)} %reshape.288), calls=%async_computation.17 | async-start | bytes 512000 | tf_op jit(solution)/shard_map/slice | solution.py:697
  512.3 9.7 %slice-start.1 = ((f32[20736]{0:T(1024)}), f32[9216]{0:T(1024)S(1)}, s32[]{:S(2)}) async-start(f32[20736]{0:T(1024)} %copy-done.15), calls=%async_computation.18 | async-start | bytes 73728 | tf_op jit(solution)/shard_map/slice | solution.py:702
  528.7 1.8 copy-start.5
  530.5 1.8 copy-start.6
  530.5 1.8 copy-start.19
  530.5 1.8 copy-start.20
  543.5 47.4 %all-to-all-start.4 = ((bf16[1,144,8,144]{1,3,0,2:T(8,128)(2,1)}), bf16[1,144,8,144]{1,3,0,2:T(8,128)(2,1)}, u32[]{:S(2)}, u32[]{:S(2)}) async-start(bf16[1,144,8,144]{1,3,0,2:T(8,128)(2,1)} %bitcast.138), calls=%async_computation.5 | async-start | bytes 1179648 | tf_op jit(solution)/shard_map/all_to_all | solution.py:635
Sparse Core Ops, SparseCore 0:
  9.6 53.1 all-gather.10
  242.3 50.8 all-reduce.9
  295.0 78.3 all-gather.14
  376.2 51.3 all-reduce.11
  429.4 37.3 all-gather.8
  468.5 38.9 all-gather.12
  509.7 31.6 reduce-scatter.7
  544.8 39.6 reduce-scatter.9
  586.9 38.3 reduce-scatter.11

commit v2 on v1

v2 whole, which is shorter than its diff:
```python
from functools import partial

import jax
import jax.numpy as jnp
from jax import lax
from jax.experimental import pallas as pl
from jax.experimental.pallas import tpu as pltpu
from jax.sharding import PartitionSpec as P

GRID = 32
SPAN = 2 * GRID - 1
STRIP = 2 * GRID * GRID
LANES = 128
BLOCK = 256
NORM_EPS = 1e-06
f32, bf16 = jnp.float32, jnp.bfloat16
GAIN_ONE, SHIFT_ONE, B_QUERY, B_VALUE, B_OUT, GAIN_TWO, SHIFT_TWO, B_DOWN = range(8)
HIGHEST = lax.Precision.HIGHEST
SCALE = 0.2
VMEM_LIMIT = 58 * 1024 * 1024


def dot(left, right, left_dim=1, right_dim=0):
    return lax.dot_general(
        left, right, (((left_dim,), (right_dim,)), ((), ())), preferred_element_type=f32
    )


def normalize(values):
    centered = values - jnp.mean(values, axis=-1, keepdims=True)
    scaled = lax.rsqrt(jnp.mean(centered * centered, axis=-1, keepdims=True) + NORM_EPS)
    return centered * scaled, scaled


def norm_back(grad_norm, normed, scaled, gain):
    inner = grad_norm * gain
    return scaled * (
        inner
        - jnp.mean(inner, axis=-1, keepdims=True)
        - normed * jnp.mean(inner * normed, axis=-1, keepdims=True)
    )


def fold_rows(values, op):
    return op(values.reshape(values.shape[0] // 8, 8, values.shape[1]), axis=0)


def strip_place(key_row):
    first = (GRID - 1 - key_row) * GRID
    return (first % LANES) // GRID, first // LANES * LANES


def widen(rows, height):
    fill = jnp.zeros((height - rows.shape[0], rows.shape[1]), rows.dtype)
    return jnp.concatenate([rows, fill], axis=0)


def rows_for(group, half, count):
    return pl.ds(pl.multiple_of((2 * group + half) * count, 16), count)


def block_of(index):
    return pl.ds(pl.multiple_of(index * BLOCK, BLOCK), BLOCK)


def build_permutation(place_ref, perm):
    length = perm.shape[0]

    def rows_of(i, carry):
        first = pl.multiple_of(i * BLOCK, BLOCK)
        spots = lax.broadcasted_iota(jnp.int32, (BLOCK, length), 0) + first
        hit = spots == place_ref[...]
        perm[pl.ds(first, BLOCK), :] = jnp.where(hit, 1.0, 0.0).astype(bf16)
        return carry

    lax.fori_loop(0, length // BLOCK, rows_of, 0)


def strips_kernel(table_ref, strips_ref):
    quarter = lax.broadcasted_iota(jnp.int32, (GRID, LANES), 1) // GRID
    per_tile = LANES // GRID

    def tile(n, carry):
        for s in range(per_tile):
            whole_tile = jnp.zeros((GRID, LANES), f32)
            for k in range(per_tile):
                row = table_ref[0, pl.ds(per_tile * n + s + k, 1), :]
                turned = pltpu.roll(
                    jnp.broadcast_to(row, (GRID, LANES)),
                    (GRID * k - GRID + 1) % LANES,
                    1,
                    stride=1,
                    stride_axis=0,
                )
                whole_tile = jnp.where(quarter == k, turned, whole_tile)
            strips_ref[0, s, :, pl.ds(pl.multiple_of(n * LANES, LANES), LANES)] = whole_tile
        return carry

    lax.fori_loop(0, STRIP // LANES, tile, 0)


def project_kernel(
    scale,
    groups,
    seq_ref,
    x_ref,
    embed_ref,
    rows_ref,
    wk_hbm,
    wq_hbm,
    tq_hbm,
    wv_hbm,
    tv_hbm,
    *refs,
):
    outs, (hat_ref, held, turned, sems) = refs[: 2 * groups], refs[2 * groups :]
    sources = (wk_hbm, wq_hbm, tq_hbm, wv_hbm, tv_hbm)
    copies = [
        pltpu.make_async_copy(source, held.at[n], sems.at[n]) for n, source in enumerate(sources)
    ]
    for copy in copies:
        copy.start()
    hat, _ = normalize(x_ref[...].astype(f32))
    hat_ref[...] = hat.astype(bf16)
    act = (hat * rows_ref[GAIN_ONE] + rows_ref[SHIFT_ONE]).astype(bf16)
    embed = jnp.broadcast_to(embed_ref[...].astype(f32), (16, embed_ref.shape[1])).astype(bf16)
    count = outs[0].shape[0] // 3
    seq = seq_ref[0]

    def put(which, value):
        turned[which] = jnp.transpose(value.astype(bf16))
        for k in range(groups):
            for h in range(2):
                outs[h * groups + k][which * count : (which + 1) * count, :] = turned[
                    which, rows_for(k ^ seq, h, count), :
                ]

    copies[0].wait()
    put(1, dot(act, held[0]))
    copies[1].wait()
    copies[2].wait()
    time_query = dot(embed, held[2])[0:1]
    put(0, (dot(act, held[1]) + time_query + rows_ref[B_QUERY]) * scale)
    copies[3].wait()
    copies[4].wait()
    time_value = dot(embed, held[4])[0:1]
    put(2, dot(act, held[3]) + time_value + rows_ref[B_VALUE])


def attend_kernel(
    head_size,
    groups,
    seq_ref,
    place_ref,
    strips_ref,
    *refs,
):
    own, outs = refs[:groups], refs[groups : 2 * groups]
    qkv_ref, expo_ref, inverse_ref, mixed_ref = refs[2 * groups : 2 * groups + 4]
    perm, by_place, query_s, key_s, value_s, scores_s = refs[2 * groups + 4 :]
    seq = seq_ref[0]
    head = pl.program_id(0)
    group, length = mixed_ref.shape
    tiles = length // BLOCK

    @pl.when(head == 0)
    def _():
        build_permutation(place_ref, perm)

        def arrange(i, carry):
            span = pl.ds(pl.multiple_of(i * BLOCK, BLOCK), BLOCK)
            part = jnp.zeros((3 * group, BLOCK), f32)
            for k in range(groups):
                part = part + dot(own[k][...], perm[span, block_of(k ^ seq)], 1, 1)
            by_place[:, span] = part
            qkv_ref[:, span] = part.astype(bf16)
            return carry

        lax.fori_loop(0, tiles, arrange, 0)

    def rows_of(which):
        first = pl.multiple_of(which * group + head * head_size, 8)
        return by_place[pl.ds(first, head_size), :]

    query_s[...] = widen(rows_of(0), LANES).astype(bf16)
    key_s[...] = jnp.transpose(widen(rows_of(1), LANES)).astype(bf16)
    value_s[...] = widen(rows_of(2), value_s.shape[0]).astype(bf16)
    own_rows = pl.ds(pl.multiple_of(head * head_size, 8), head_size)

    def tile(t, carry):
        first = pl.multiple_of(t * BLOCK, BLOCK)
        span = pl.ds(first, BLOCK)
        query = query_s[:, span]
        peak = jnp.full((8, BLOCK), -jnp.inf, f32)
        for c in range(tiles):
            keys = slice(c * BLOCK, (c + 1) * BLOCK)
            pieces = []
            for key_row in range(c * BLOCK // GRID, (c + 1) * BLOCK // GRID):
                shift, start = strip_place(key_row)
                pieces.append(strips_ref[0, shift, :, pl.ds(first + start, BLOCK)])
            scores = dot(key_s[keys, :], query) + jnp.concatenate(pieces, axis=0)
            scores_s[keys, :] = scores
            peak = jnp.maximum(peak, fold_rows(scores, jnp.max))
        peak = jnp.max(peak, axis=0, keepdims=True)
        total = jnp.zeros((8, BLOCK), f32)
        mixed = jnp.zeros((value_s.shape[0], BLOCK), f32)
        for c in range(tiles):
            keys = slice(c * BLOCK, (c + 1) * BLOCK)
            expo = jnp.exp(scores_s[keys, :] - peak)
            total = total + fold_rows(expo, jnp.sum)
            low = expo.astype(bf16)
            expo_ref[0, keys, span] = low
            mixed = mixed + dot(value_s[:, keys], low)
        inverse = 1.0 / jnp.sum(total, axis=0, keepdims=True)
        inverse_ref[0, :, span] = inverse
        mixed_ref[own_rows, span] = (mixed * inverse)[:head_size]
        return carry

    lax.fori_loop(0, tiles, tile, 0)

    @pl.when(head == pl.num_programs(0) - 1)
    def _():
        low = mixed_ref[...].astype(bf16)
        for k in range(groups):
            outs[k][...] = dot(low, perm[:, block_of(k ^ seq)]).astype(bf16)


def attend_back_kernel(
    head_size,
    groups,
    seq_ref,
    qkv_ref,
    expo_ref,
    inverse_ref,
    mixed_ref,
    place_ref,
    *refs,
):
    given, outs = refs[:groups], refs[groups : 2 * groups]
    (
        strips_ref,
        perm,
        by_place,
        grad_place,
        grads,
        query_s,
        key_s,
        value_s,
        grad_s,
        grad_t,
        offset_s,
        grad_key,
        grad_value,
    ) = refs[2 * groups :]
    seq = seq_ref[0]
    head = pl.program_id(0)
    group, length = mixed_ref.shape
    tiles = length // BLOCK
    scale = head_size ** (-0.5)

    @pl.when(head == 0)
    def _():
        build_permutation(place_ref, perm)

        def arrange(i, carry):
            span = pl.ds(pl.multiple_of(i * BLOCK, BLOCK), BLOCK)
            part = jnp.zeros((group, BLOCK), f32)
            for k in range(groups):
                part = part + dot(given[k][...], perm[span, block_of(k ^ seq)], 1, 1)
            grad_place[:, span] = part
            by_place[:, span] = qkv_ref[:, span].astype(f32)
            return carry

        lax.fori_loop(0, tiles, arrange, 0)

    own_rows = pl.ds(pl.multiple_of(head * head_size, 8), head_size)

    def rows_of(which):
        first = pl.multiple_of(which * group + head * head_size, 8)
        return by_place[pl.ds(first, head_size), :]

    query_s[...] = jnp.transpose(widen(rows_of(0), LANES)).astype(bf16)
    key_s[...] = widen(rows_of(1), key_s.shape[0]).astype(bf16)
    value_s[...] = jnp.transpose(widen(rows_of(2), LANES)).astype(bf16)
    grad = grad_place[own_rows, :]
    inverse = inverse_ref[0]
    offset_s[...] = inverse * jnp.sum(grad * mixed_ref[own_rows, :], axis=0, keepdims=True)
    grad = widen(grad * inverse, LANES)
    grad_s[...] = grad.astype(bf16)
    grad_t[...] = jnp.transpose(grad).astype(bf16)
    grad_key[...] = jnp.zeros_like(grad_key)
    grad_value[...] = jnp.zeros_like(grad_value)
    strips_ref[...] = jnp.zeros_like(strips_ref)

    def tile(t, carry):
        first = pl.multiple_of(t * BLOCK, BLOCK)
        span = pl.ds(first, BLOCK)
        grad_tile = grad_s[:, span]
        offset = offset_s[:, span]
        grad_query = jnp.zeros((key_s.shape[0], BLOCK), f32)
        for c in range(tiles):
            keys = slice(c * BLOCK, (c + 1) * BLOCK)
            expo = expo_ref[0, keys, span]
            grad_scores = expo.astype(f32) * (dot(value_s[keys, :], grad_tile) - offset)
            for row in range(BLOCK // GRID):
                shift, start = strip_place(c * BLOCK // GRID + row)
                strips_ref[0, shift, :, pl.ds(first + start, BLOCK)] += grad_scores[
                    row * GRID : (row + 1) * GRID
                ]
            low = grad_scores.astype(bf16)
            grad_query = grad_query + dot(key_s[:, keys], low)
            grad_key[keys, :] += dot(low, query_s[span, :])
            grad_value[keys, :] += dot(expo, grad_t[span, :])
        grads[own_rows, span] = grad_query[:head_size] * scale
        return carry

    lax.fori_loop(0, tiles, tile, 0)
    for which, total in ((1, grad_key), (2, grad_value)):
        first = pl.multiple_of(which * group + head * head_size, 8)
        grads[pl.ds(first, head_size), :] = jnp.transpose(total[...])[:head_size]

    @pl.when(head == pl.num_programs(0) - 1)
    def _():
        low = grads[...].astype(bf16)
        for k in range(groups):
            outs[k][...] = dot(low, perm[:, block_of(k ^ seq)]).astype(bf16)


def mlp_first_kernel(
    groups,
    step,
    seq_ref,
    x_ref,
    dy_ref,
    rows_ref,
    b_up_ref,
    w_out_hbm,
    w_up_hbm,
    w_down_hbm,
    *refs,
):
    given = refs[: 2 * groups]
    act_hbm, act_t_hbm, inner_hbm, norm_t_ref, mixed_t_ref, middle_ref, up_sum_ref = refs[
        2 * groups : 2 * groups + 7
    ]
    (
        w_out_s,
        w_up_s,
        w_down_s,
        act_s,
        act_t_s,
        inner_s,
        norm_s,
        sem,
        up_sems,
        down_sems,
        act_sems,
        act_t_sems,
        inner_sems,
    ) = refs[2 * groups + 7 :]
    chunks = w_up_s.shape[0]
    seq = seq_ref[0]

    def span_of(i):
        return pl.ds(pl.multiple_of(i * step, step), step)

    def fetch(i):
        return (
            pltpu.make_async_copy(w_up_hbm.at[:, span_of(i)], w_up_s.at[i], up_sems.at[i]),
            pltpu.make_async_copy(w_down_hbm.at[span_of(i), :], w_down_s.at[i], down_sems.at[i]),
        )

    def put(i):
        return (
            pltpu.make_async_copy(act_s.at[i], act_hbm.at[:, span_of(i)], act_sems.at[i]),
            pltpu.make_async_copy(act_t_s.at[i], act_t_hbm.at[span_of(i), :], act_t_sems.at[i]),
            pltpu.make_async_copy(inner_s.at[i], inner_hbm.at[:, span_of(i)], inner_sems.at[i]),
        )

    def begin(i, carry):
        for copy in fetch(i):
            copy.start()
        return carry

    out_copy = pltpu.make_async_copy(w_out_hbm, w_out_s, sem.at[0])
    out_copy.start()
    lax.fori_loop(0, chunks, begin, 0)
    count = given[0].shape[0]
    for k in range(groups):
        for h in range(2):
            mixed_t_ref[rows_for(k ^ seq, h, count), :] = given[h * groups + k][...]
    mixed = jnp.transpose(mixed_t_ref[...])
    out_copy.wait()
    middle = x_ref[...].astype(f32) + dot(mixed, w_out_s[...]) + rows_ref[B_OUT]
    hat, _ = normalize(middle)
    middle_ref[...] = middle
    norm = (hat * rows_ref[GAIN_TWO] + rows_ref[SHIFT_TWO]).astype(bf16)
    norm_s[...] = norm
    norm_t_ref[...] = jnp.transpose(norm)

    def chunk(i, carry):
        for copy in fetch(i):
            copy.wait()
        inner = dot(norm_s[...], w_up_s[i]) + b_up_ref[:, span_of(i)]
        cdf = 0.5 * (1.0 + lax.erf(inner * (0.5**0.5)))
        pdf = jnp.exp(-0.5 * inner * inner) * 0.3989422804014327
        act = (inner * cdf).astype(bf16)
        low = (dot(dy_ref[...], w_down_s[i], 1, 1) * (cdf + inner * pdf)).astype(bf16)
        act_s[i] = act
        act_t_s[i] = jnp.transpose(act)
        inner_s[i] = low
        up_sum_ref[:, span_of(i)] = jnp.sum(low.astype(f32), axis=0, keepdims=True)
        for copy in put(i):
            copy.start()
        return carry

    lax.fori_loop(0, chunks, chunk, 0)

    def finish(i, carry):
        for copy in put(i):
            copy.wait()
        return carry

    lax.fori_loop(0, chunks, finish, 0)


def mlp_second_kernel(
    groups,
    step,
    seq_ref,
    middle_ref,
    dy_ref,
    rows_ref,
    act_ref,
    inner_ref,
    w_out_hbm,
    w_up_hbm,
    w_down_hbm,
    *refs,
):
    outs = refs[: 2 * groups]
    result_ref, grad_middle_ref, branch_ref, sums_ref = refs[2 * groups : 2 * groups + 4]
    (
        w_out_s,
        w_up_s,
        w_down_s,
        result_s,
        grad_s,
        mixed_s,
        sem,
        up_sems,
        down_sems,
    ) = refs[2 * groups + 4 :]
    chunks = w_up_s.shape[0]
    seq = seq_ref[0]

    def span_of(i):
        return pl.ds(pl.multiple_of(i * step, step), step)

    def fetch(i):
        return (
            pltpu.make_async_copy(w_up_hbm.at[:, span_of(i)], w_up_s.at[i], up_sems.at[i]),
            pltpu.make_async_copy(w_down_hbm.at[span_of(i), :], w_down_s.at[i], down_sems.at[i]),
        )

    def begin(i, carry):
        for copy in fetch(i):
            copy.start()
        return carry

    lax.fori_loop(0, chunks, begin, 0)
    out_copy = pltpu.make_async_copy(w_out_hbm, w_out_s, sem.at[0])
    out_copy.start()
    result_s[...] = middle_ref[...] + rows_ref[B_DOWN]
    grad_s[...] = jnp.zeros_like(grad_s)

    def chunk(i, carry):
        for copy in fetch(i):
            copy.wait()
        result_s[...] += dot(act_ref[:, span_of(i)], w_down_s[i])
        grad_s[...] += dot(inner_ref[:, span_of(i)], w_up_s[i], 1, 1)
        return carry

    lax.fori_loop(0, chunks, chunk, 0)
    result_ref[...] = result_s[...].astype(bf16)
    hat, scaled = normalize(middle_ref[...])
    dy = dy_ref[...].astype(f32)
    grad_norm = grad_s[...]
    grad_middle = dy + norm_back(grad_norm, hat, scaled, rows_ref[GAIN_TWO])
    branch = grad_middle.astype(bf16)
    grad_middle_ref[...] = grad_middle
    branch_ref[...] = branch
    out_copy.wait()
    mixed_s[...] = dot(w_out_s[...], branch, 1, 1).astype(bf16)
    count = outs[0].shape[0]
    for k in range(groups):
        for h in range(2):
            outs[h * groups + k][...] = mixed_s[rows_for(k ^ seq, h, count), :]
    sums_ref[...] = jnp.concatenate(
        [
            jnp.sum(dy, axis=0, keepdims=True),
            jnp.sum(grad_norm * hat, axis=0, keepdims=True),
            jnp.sum(grad_norm, axis=0, keepdims=True),
            jnp.sum(branch.astype(f32), axis=0, keepdims=True),
            jnp.zeros((4, dy.shape[1]), f32),
        ],
        axis=0,
    )


def up_grad_kernel(
    order_ref, own_ref, other_ref, inner_ref, inner_other, keep_0, send_0, keep_1, send_1
):
    step = pl.program_id(0)
    total = dot(own_ref[0], inner_ref[...]) + dot(other_ref[0], inner_other[...])
    low = total.astype(bf16)
    half = low.shape[0] // 2
    first = step < pl.num_programs(0) // 2

    @pl.when(first)
    def _():
        keep_0[0], send_0[0] = low[:half], low[half:]

    @pl.when(jnp.logical_not(first))
    def _():
        keep_1[0], send_1[0] = low[:half], low[half:]


def down_grad_kernel(act_ref, dy_ref, out_ref, total_s):
    source = pl.program_id(0)
    part = dot(act_ref[0], dy_ref[0])

    @pl.when(source == 0)
    def _():
        total_s[...] = part

    @pl.when(source > 0)
    def _():
        total_s[...] += part

    @pl.when(source == pl.num_programs(0) - 1)
    def _():
        out_ref[...] = jnp.transpose(total_s[...].astype(bf16))


def qkv_grad_kernel(groups, seq_ref, hat_ref, weight_ref, rows_ref, *refs):
    given, (out_ref, sums_ref, norms_ref) = refs[: 2 * groups], refs[2 * groups :]
    seq = seq_ref[0]
    count = given[0].shape[0]
    gain, shift = rows_ref[GAIN_ONE], rows_ref[SHIFT_ONE]
    norms = jnp.zeros(norms_ref.shape, f32)
    for h in range(2):
        span = slice(h * count, (h + 1) * count)
        product = jnp.zeros((count, hat_ref.shape[2]), f32)
        sums = jnp.zeros((count, 1), f32)
        for k in range(groups):
            grads = given[h * groups + k][...]
            product = product + dot(grads, hat_ref[k ^ seq])
            sums = sums + jnp.sum(grads.astype(f32), axis=1, keepdims=True)
        weight = weight_ref[span, :].astype(f32)
        norms = norms + jnp.concatenate(
            [
                jnp.sum(weight * product, axis=0, keepdims=True),
                jnp.sum(weight * sums, axis=0, keepdims=True),
                jnp.zeros((6, weight.shape[1]), f32),
            ],
            axis=0,
        )
        sums_ref[span, :] = sums
        out_ref[h] = jnp.transpose((product * gain + sums * shift).astype(bf16))
    norms_ref[...] = norms


def tokens_kernel(groups, seq_ref, x_ref, middle_ref, rows_ref, wq_hbm, wk_hbm, wv_hbm, *refs):
    given, (out_ref, held, grads_s, sems) = refs[: 2 * groups], refs[2 * groups :]
    copies = [
        pltpu.make_async_copy(source, held.at[n], sems.at[n])
        for n, source in enumerate((wq_hbm, wk_hbm, wv_hbm))
    ]
    for copy in copies:
        copy.start()
    seq = seq_ref[0]
    count = given[0].shape[0] // 3
    for k in range(groups):
        for h in range(2):
            for which in range(3):
                grads_s[which, rows_for(k ^ seq, h, count), :] = given[h * groups + k][
                    which * count : (which + 1) * count
                ]
    hat, scaled = normalize(x_ref[...].astype(f32))
    total = jnp.zeros(middle_ref.shape, f32)
    for which, copy in enumerate(copies):
        grads = jnp.transpose(grads_s[which])
        copy.wait()
        total = total + dot(grads, held[which], 1, 1)
    out_ref[...] = (
        middle_ref[...] + norm_back(total, hat, scaled, rows_ref[GAIN_ONE])
    ).astype(bf16)


def whole(shape):
    zeros = (0,) * len(shape)
    return pl.BlockSpec(shape, lambda s: zeros, pipeline_mode=pl.Buffered(1))


def kept(shape):
    zeros = (0,) * len(shape)
    return pl.BlockSpec(shape, lambda s: zeros)


def per_head(shape):
    rest = (0,) * (len(shape) - 1)
    return pl.BlockSpec((1,) + tuple(shape[1:]), lambda s: (s,) + rest)


def params(grid=True):
    return pltpu.CompilerParams(
        dimension_semantics=("arbitrary",) if grid else None, vmem_limit_bytes=VMEM_LIMIT
    )


def takes(microseconds):
    return pl.CostEstimate(
        flops=int(microseconds * SCALE * 1e9), bytes_accessed=int(microseconds * SCALE * 3e6), transcendentals=0
    )


IN_VMEM = pl.BlockSpec(memory_space=pltpu.VMEM)
IN_SMEM = pl.BlockSpec(memory_space=pltpu.SMEM)
IN_HBM = pl.BlockSpec(memory_space=pl.ANY)


def shape_of(shape, kind):
    return jax.ShapeDtypeStruct(shape, kind)


def bias_strips(table):
    heads = table.shape[0]
    out = shape_of((heads, LANES // GRID, GRID, STRIP), f32)
    return pl.pallas_call(
        strips_kernel,
        grid=(heads,),
        in_specs=[per_head(table.shape)],
        out_specs=per_head(out.shape),
        out_shape=out,
        compiler_params=params(),
        cost_estimate=takes(9),
        name="strips",
    )(table)


def project(seq, x, embed, rows, weights, groups, scale):
    count, width = x.shape
    part = shape_of((3 * width // groups // 2, count), bf16)
    outs = pl.pallas_call(
        partial(project_kernel, scale, groups),
        in_specs=[IN_SMEM] + [IN_VMEM] * 3 + [IN_HBM] * 5,
        out_specs=[IN_VMEM] * (2 * groups + 1),
        out_shape=(part,) * (2 * groups) + (shape_of((count, width), bf16),),
        scratch_shapes=[
            pltpu.VMEM((5, width, width), bf16),
            pltpu.VMEM((3, width, count), bf16),
            pltpu.SemaphoreType.DMA((5,)),
        ],
        compiler_params=params(False),
        cost_estimate=takes(9),
        name="project",
    )(seq, x, embed, rows, *weights)
    return outs[:groups], outs[groups : 2 * groups], outs[2 * groups]


def attend(seq, own, place, strips, half, head_size):
    heads = strips.shape[0] // 2
    length = place.shape[1]
    group = heads * head_size
    groups = len(own)
    tall = -(-head_size // 16) * 16
    saved = (
        shape_of((3 * group, length), bf16),
        shape_of((heads, length, length), bf16),
        shape_of((heads, 1, length), f32),
        shape_of((group, length), f32),
    )
    own_strips = pl.BlockSpec(
        (1,) + strips.shape[1:], lambda s: (half * heads + s, 0, 0, 0)
    )
    outs = pl.pallas_call(
        partial(attend_kernel, head_size, groups),
        grid=(heads,),
        in_specs=[IN_SMEM, whole(place.shape), own_strips] + [whole(a.shape) for a in own],
        out_specs=[kept((group, BLOCK))] * groups
        + [
            kept(saved[0].shape),
            per_head(saved[1].shape),
            per_head(saved[2].shape),
            kept(saved[3].shape),
        ],
        out_shape=(shape_of((group, BLOCK), bf16),) * groups + saved,
        scratch_shapes=[
            pltpu.VMEM((length, length), bf16),
            pltpu.VMEM((3 * group, length), f32),
            pltpu.VMEM((LANES, length), bf16),
            pltpu.VMEM((length, LANES), bf16),
            pltpu.VMEM((tall, length), bf16),
            pltpu.VMEM((length, BLOCK), f32),
        ],
        compiler_params=params(),
        cost_estimate=takes(13),
        name="attend",
    )(seq, place, strips, *own)
    return outs[:groups], outs[groups:]


def attend_back(seq, grad_mixed, qkv, expo, inverse, mixed, place, head_size):
    heads, length, _ = expo.shape
    group = heads * head_size
    groups = len(grad_mixed)
    tall = -(-head_size // 16) * 16
    strips = shape_of((heads, LANES // GRID, GRID, STRIP), f32)
    outs = pl.pallas_call(
        partial(attend_back_kernel, head_size, groups),
        grid=(heads,),
        in_specs=[
            IN_SMEM,
            whole(qkv.shape),
            per_head(expo.shape),
            per_head(inverse.shape),
            whole(mixed.shape),
            whole(place.shape),
        ]
        + [whole(a.shape) for a in grad_mixed],
        out_specs=[kept((3 * group, BLOCK))] * groups + [per_head(strips.shape)],
        out_shape=(shape_of((3 * group, BLOCK), bf16),) * groups + (strips,),
        scratch_shapes=[
            pltpu.VMEM((length, length), bf16),
            pltpu.VMEM((3 * group, length), f32),
            pltpu.VMEM((group, length), f32),
            pltpu.VMEM((3 * group, length), f32),
            pltpu.VMEM((length, LANES), bf16),
            pltpu.VMEM((tall, length), bf16),
            pltpu.VMEM((length, LANES), bf16),
            pltpu.VMEM((LANES, length), bf16),
            pltpu.VMEM((length, LANES), bf16),
            pltpu.VMEM((1, length), f32),
            pltpu.VMEM((length, LANES), f32),
            pltpu.VMEM((length, LANES), f32),
        ],
        compiler_params=params(),
        cost_estimate=takes(16),
        name="attend_back",
    )(seq, qkv, expo, inverse, mixed, place, *grad_mixed)
    return outs[:groups], outs[groups]


def mlp_first(seq, mixed, x, dy, rows, b_up, w_out, w_up, w_down):
    count, width = x.shape
    hidden = w_up.shape[1]
    step = 512
    chunks = hidden // step
    dma = pltpu.SemaphoreType.DMA
    return pl.pallas_call(
        partial(mlp_first_kernel, len(mixed) // 2, step),
        in_specs=[IN_SMEM] + [IN_VMEM] * 4 + [IN_HBM] * 3 + [IN_VMEM] * len(mixed),
        out_specs=[IN_HBM] * 3 + [IN_VMEM] * 4,
        out_shape=(
            shape_of((count, hidden), bf16),
            shape_of((hidden, count), bf16),
            shape_of((count, hidden), bf16),
            shape_of((width, count), bf16),
            shape_of((width, count), bf16),
            shape_of((count, width), f32),
            shape_of((1, hidden), f32),
        ),
        scratch_shapes=[
            pltpu.VMEM((width, width), bf16),
            pltpu.VMEM((chunks, width, step), bf16),
            pltpu.VMEM((chunks, step, width), bf16),
            pltpu.VMEM((chunks, count, step), bf16),
            pltpu.VMEM((chunks, step, count), bf16),
            pltpu.VMEM((chunks, count, step), bf16),
            pltpu.VMEM((count, width), bf16),
            dma((1,)),
        ]
        + [dma((chunks,))] * 5,
        compiler_params=params(False),
        cost_estimate=takes(14),
        name="mlp_first",
    )(seq, x, dy, rows, b_up, w_out, w_up, w_down, *mixed)


def mlp_second(seq, middle, dy, rows, act, inner, w_out, w_up, w_down, groups):
    count, width = middle.shape
    hidden = w_up.shape[1]
    step = 512
    chunks = hidden // step
    part = shape_of((width // groups // 2, count), bf16)
    dma = pltpu.SemaphoreType.DMA
    outs = pl.pallas_call(
        partial(mlp_second_kernel, groups, step),
        in_specs=[IN_SMEM] + [IN_VMEM] * 5 + [IN_HBM] * 3,
        out_specs=[IN_VMEM] * (2 * groups + 4),
        out_shape=(part,) * (2 * groups)
        + (
            shape_of((count, width), bf16),
            shape_of((count, width), f32),
            shape_of((count, width), bf16),
            shape_of((8, width), f32),
        ),
        scratch_shapes=[
            pltpu.VMEM((width, width), bf16),
            pltpu.VMEM((chunks, width, step), bf16),
            pltpu.VMEM((chunks, step, width), bf16),
            pltpu.VMEM((count, width), f32),
            pltpu.VMEM((count, width), f32),
            pltpu.VMEM((width, count), bf16),
            dma((1,)),
            dma((chunks,)),
            dma((chunks,)),
        ],
        compiler_params=params(False),
        cost_estimate=takes(14),
        name="mlp_second",
    )(seq, middle, dy, rows, act, inner, w_out, w_up, w_down)
    return outs[:groups], outs[groups : 2 * groups], outs[2 * groups :]


def up_grad(order, own, other, inner, inner_other):
    _, rows, count = own.shape
    groups = order.shape[0]
    width = inner.shape[1] // groups
    side = groups // 2
    wide = pl.BlockSpec((count, width), lambda s, order_ref: (0, order_ref[s]))
    left = pl.BlockSpec((1, rows, count), lambda s, order_ref: (s // side, 0, 0))
    block = (1, rows // 2, width)
    early = pl.BlockSpec(block, lambda s, order_ref: (jnp.minimum(s, side - 1), 0, 0))
    late = pl.BlockSpec(block, lambda s, order_ref: (jnp.maximum(s - side, 0), 0, 0))
    return pl.pallas_call(
        up_grad_kernel,
        grid_spec=pltpu.PrefetchScalarGridSpec(
            num_scalar_prefetch=1,
            grid=(groups,),
            in_specs=[left, left, wide, wide],
            out_specs=[early, early, late, late],
        ),
        out_shape=(shape_of((side, rows // 2, width), bf16),) * 4,
        compiler_params=params(),
        cost_estimate=takes(8),
        name="up_grad",
    )(order, own, other, inner, inner_other)


def down_grad(act, dy):
    sources, rows, _ = act.shape
    width = dy.shape[2]
    return pl.pallas_call(
        down_grad_kernel,
        grid=(sources,),
        in_specs=[per_head(act.shape), per_head(dy.shape)],
        out_specs=kept((width, rows)),
        out_shape=shape_of((width, rows), bf16),
        scratch_shapes=[pltpu.VMEM((rows, width), f32)],
        compiler_params=params(),
        cost_estimate=takes(8),
        name="down_grad",
    )(act, dy)


def qkv_grad(seq, grads, hat, weight, rows):
    count, width = weight.shape
    return pl.pallas_call(
        partial(qkv_grad_kernel, len(grads) // 2),
        in_specs=[IN_SMEM] + [IN_VMEM] * (3 + len(grads)),
        out_specs=[IN_VMEM] * 3,
        out_shape=(
            shape_of((2, width, count // 2), bf16),
            shape_of((count, 1), f32),
            shape_of((8, width), f32),
        ),
        compiler_params=params(False),
        cost_estimate=takes(9),
        name="qkv_grad",
    )(seq, hat, weight, rows, *grads)


def token_grad(seq, grads, x, middle, rows, weights):
    count, width = x.shape
    return pl.pallas_call(
        partial(tokens_kernel, len(grads) // 2),
        in_specs=[IN_SMEM] + [IN_VMEM] * 3 + [IN_HBM] * 3 + [IN_VMEM] * len(grads),
        out_specs=IN_VMEM,
        out_shape=shape_of((count, width), bf16),
        scratch_shapes=[
            pltpu.VMEM((3, width, width), bf16),
            pltpu.VMEM((3, width, count), bf16),
            pltpu.SemaphoreType.DMA((3,)),
        ],
        compiler_params=params(False),
        cost_estimate=takes(9),
        name="token_grad",
    )(seq, x, middle, rows, *weights, *grads)


def exchange(array, axis, step):
    size = lax.axis_size(axis)
    return lax.ppermute(array, axis, [(i, i ^ step) for i in range(size)])


def sum_over(vector, axis):
    step = 1
    while step < lax.axis_size(axis):
        vector = vector + exchange(vector, axis, step)
        step *= 2
    return vector


def gather_rows(vector, axis):
    size, index = lax.axis_size(axis), lax.axis_index(axis)
    rows = vector[None]
    step = 1
    while step < size:
        rows = jnp.concatenate([rows, exchange(rows, axis, step)], axis=0)
        step *= 2
    return jnp.concatenate(
        [lax.dynamic_index_in_dim(rows, n ^ index, 0) for n in range(size)], axis=0
    )


def swap(parts, axis):
    return [parts[0]] + [exchange(parts[k], axis, k) for k in range(1, len(parts))]


def halve(array, axis, dim, step, bit):
    keep = lax.dynamic_index_in_dim(array, bit, dim, keepdims=False)
    send = lax.dynamic_index_in_dim(array, 1 - bit, dim, keepdims=False)
    return (keep.astype(f32) + exchange(send, axis, step).astype(f32)).astype(bf16)


def halve_bits(array, dim, bits, order):
    index = lax.axis_index("dp")
    left = sorted(bits, reverse=True)
    for bit in order:
        array = halve(array, "dp", dim + left.index(bit), 1 << bit, (index >> bit) & 1)
        left.remove(bit)
    return array


def add_low(left, right):
    return (left.astype(f32) + right.astype(f32)).astype(bf16)


def two_halves(keep, received, dim):
    size = keep.shape[dim] // 2
    return [
        add_low(*(lax.slice_in_dim(a, n * size, (n + 1) * size, axis=dim) for a in (keep, received)))
        for n in range(2)
    ]


def tie(*arrays):
    return lax.optimization_barrier(arrays)


def key_places(rel_index):
    first = rel_index[0]
    top = jnp.max(first)
    row = top // SPAN - first // SPAN
    column = top % SPAN - first % SPAN
    return (row * GRID + column)[None, :].astype(jnp.int32)


def table_grad(strips):
    heads = strips.shape[0]
    total = sum(
        jnp.pad(strips[:, s], ((0, 0), (0, 0), (s * GRID, LANES - s * GRID)))
        for s in range(LANES // GRID)
    )
    parts = total[:, :, : SPAN * GRID].reshape(heads, GRID, SPAN, GRID)
    sides = jnp.arange(GRID, dtype=jnp.int32)
    place = GRID - 1 - sides[:, None] + sides[None, :]
    onehot = (place[:, :, None] == jnp.arange(SPAN, dtype=jnp.int32)).astype(f32)
    return jnp.einsum("hjai,jib->hab", parts, onehot, precision=HIGHEST).reshape(
        heads, SPAN * SPAN
    )


def per_device(
    tokens,
    timesteps,
    rel_index,
    time_table,
    bias_table,
    gain_one,
    shift_one,
    w_query,
    w_key,
    w_value,
    t_query,
    t_value,
    b_query,
    b_value,
    w_out,
    b_out,
    gain_two,
    shift_two,
    w_up,
    b_up,
    w_down,
    b_down,
    cotangent,
):
    _, local, width = tokens.shape
    hidden = w_up.shape[1]
    heads = bias_table.shape[0]
    head_size = width // heads
    n_dp, n_seq = lax.axis_size("dp"), lax.axis_size("seq")
    dp, seq = lax.axis_index("dp"), lax.axis_index("seq")
    own_heads = heads // n_seq
    group = own_heads * head_size
    half = group // 2
    scale = head_size ** (-0.5)
    table_rows = time_table.shape[0]
    down_rows, out_rows = hidden // n_dp, width // n_dp

    def own_columns(array):
        return lax.dynamic_slice_in_dim(array, seq * group, group, axis=array.ndim - 1)

    x, dy = tokens[0], cotangent[0]
    rows = jnp.stack(
        [gain_one, shift_one, b_query, b_value, b_out, gain_two, shift_two, b_down]
    )[:, None]
    here = seq.astype(jnp.int32)[None]
    embed = lax.dynamic_slice_in_dim(time_table, timesteps[0], 1, 0)
    *mine, hat_one = project(
        here, x, embed, rows, (w_key, w_query, t_query, w_value, t_value), n_seq, scale
    )
    mine = [swap(parts, "seq") for parts in mine]
    dy_all = lax.all_gather(dy, "dp", axis=0)
    place = key_places(rel_index)
    table = lax.dynamic_slice_in_dim(bias_table, seq * own_heads, own_heads, 0)
    table = jnp.pad(
        table.reshape(own_heads, SPAN, SPAN), ((0, 0), (0, 72 - SPAN), (0, LANES - SPAN))
    )
    table, hat_one = tie(table, hat_one)
    strips = bias_strips(table)
    weight = jnp.concatenate([own_columns(w).T for w in (w_query, w_key, w_value)], axis=0)
    weight = jnp.swapaxes(weight.reshape(3, 2, half, width), 0, 1).reshape(6 * half, width)
    place, dy_all, weight = tie(place, dy_all, weight)
    tokens_0, saved_0 = attend(here, mine[0], place, strips, 0, head_size)
    mine_1, hat_one, tokens_0, place = tie(mine[1], hat_one, tokens_0, place)
    mixed_0 = swap(tokens_0, "seq")
    hat_all = lax.all_gather(hat_one, "seq", axis=0)
    tokens_1, saved_1 = attend(here, mine_1, place, strips, 1, head_size)
    mixed_1 = swap(tokens_1, "seq")
    act, act_t, grad_inner, norm_t, mixed_t, middle, up_sum = mlp_first(
        here, mixed_0 + mixed_1, x, dy, rows, b_up[None], w_out, w_up, w_down
    )

    chip, core = dp // 2, dp % 2
    by_core = norm_t.reshape(n_dp // 2, 2, out_rows, local)

    dp_bits = list(range(n_dp.bit_length() - 1))
    chip_bits = dp_bits[1:]
    bits = len(chip_bits)
    turned_bits = [sum(((n >> b) & 1) << (bits - 1 - b) for b in range(bits)) for n in range(1 << bits)]
    orders = [chip_bits, chip_bits[::-1]]
    places = jnp.stack([jnp.array(turned_bits), jnp.arange(1 << bits)]) ^ chip

    def rows_of(core):
        own = lax.dynamic_index_in_dim(by_core, core, 1, keepdims=False)
        return jnp.take(own, places, axis=0).reshape(2, width // 2, local)

    norm_other = exchange(rows_of(1 - core), "dp", 1)
    inner_other = exchange(grad_inner, "dp", 1)
    seq_order = (jnp.arange(n_seq) ^ seq).astype(jnp.int32)
    up_parts = up_grad(seq_order, rows_of(core), norm_other, grad_inner, inner_other)
    act_parts = lax.all_to_all(act_t.reshape(n_dp, down_rows, local), "dp", 0, 0)
    middle, dy_all, up_parts = tie(middle, dy_all, up_parts)
    grad_0, grad_1, (result, grad_middle, branch, sums_two) = mlp_second(
        here, middle, dy, rows, act, grad_inner, w_out, w_up, w_down, n_seq
    )
    out_part = dot(mixed_t, branch).astype(bf16)
    grad_0, grad_1 = swap(grad_0, "seq"), swap(grad_1, "seq")
    part_down = down_grad(act_parts, dy_all)
    part_down, grad_0 = tie(part_down, grad_0)
    grad_w_down = lax.psum_scatter(part_down, "seq", scatter_dimension=0, tiled=True)
    grads_0, strips_0 = attend_back(here, grad_0, *saved_0, place, head_size)
    grads_0, grad_1 = tie(grads_0, grad_1)
    heads_0 = swap(grads_0, "seq")
    halves = [
        two_halves(keep, exchange(send, "dp", 1 << o[0]), 1)
        for keep, send, o in zip(up_parts[::2], up_parts[1::2], orders)
    ]
    halves, grad_1 = tie(halves, grad_1)
    grads_1, strips_1 = attend_back(here, grad_1, *saved_1, place, head_size)
    heads_1 = swap(grads_1, "seq")
    for n in range(1, bits):
        halves = [
            two_halves(keep, exchange(send, "dp", 1 << o[n]), 1 if n + 1 < bits else 0)
            for (keep, send), o in zip(halves, orders)
        ]
    halves, weight, grads_1 = tie(halves, weight, grads_1)
    product, sums_one, norms = qkv_grad(here, list(grads_0) + list(grads_1), hat_all, weight, rows)
    near = [add_low(keep, exchange(send, "seq", 1)) for keep, send in halves]
    grad_w_up = (near[0].astype(f32) + exchange(near[1], "seq", 2).astype(f32))[0]
    grad_w_down = jnp.transpose(grad_w_down).astype(f32)

    bits_shape = (2,) * len(dp_bits)
    grad_qkv = halve_bits(
        product.reshape((2,) + bits_shape + (out_rows, 3 * half)), 1, dp_bits, dp_bits
    )
    grad_qkv = grad_qkv.astype(f32).reshape(2, out_rows, 3, half)
    grad_qkv = jnp.transpose(grad_qkv, (1, 2, 0, 3)).reshape(out_rows, 3, group)
    out_part = halve_bits(
        out_part.reshape(bits_shape + (out_rows, width)), 0, dp_bits, dp_bits[:1] + dp_bits[:0:-1]
    )
    out_part = jnp.swapaxes(out_part.reshape(out_rows, n_seq, group), 0, 1)
    grad_w_out = jnp.sum(lax.all_to_all(out_part, "seq", 0, 0).astype(f32), axis=0)
    grad_tokens = token_grad(
        here, heads_0 + heads_1, x, grad_middle, rows, (w_query, w_key, w_value)
    )

    sums_one = jnp.swapaxes(sums_one.reshape(2, 3, half), 0, 1).reshape(3, group)
    query_sum, value_sum = sums_one[0], sums_one[2]
    tq_own, tv_own = own_columns(t_query), own_columns(t_value)
    grad_embed = jnp.dot(tq_own.astype(f32), query_sum, precision=HIGHEST) + jnp.dot(
        tv_own.astype(f32), value_sum, precision=HIGHEST
    )
    own_image = lax.broadcasted_iota(jnp.int32, (n_dp, 1), 0) == dp

    def slot(row):
        return jnp.where(own_image, row[None, :], 0.0).reshape(-1)

    apart = [table_grad(jnp.concatenate([strips_0, strips_1])).reshape(-1), query_sum, value_sum]
    summed = [
        slot(grad_embed),
        up_sum[0],
        sums_two[:4].reshape(-1),
        norms[:2].reshape(-1),
    ]
    images = [slot(jnp.concatenate([query_sum, value_sum, timesteps.astype(f32)]))]
    sizes = [sum(a.shape[0] for a in part) for part in (apart, summed, images)]
    vector = sum_over(jnp.concatenate(apart + summed + images), "dp")
    image_sums = vector[sizes[0] + sizes[1] :].reshape(n_dp, 2 * group + 1)
    steps_all = image_sums[:, 2 * group].astype(jnp.int32)
    vector = gather_rows(vector[: sizes[0] + sizes[1]], "seq")
    table_size = own_heads * SPAN * SPAN
    grad_bias_table = vector[:, :table_size].reshape(heads, SPAN * SPAN)
    grad_b_query = vector[:, table_size : table_size + group].reshape(-1)
    grad_b_value = vector[:, table_size + group : sizes[0]].reshape(-1)
    both = jnp.sum(vector[:, sizes[0] :], axis=0)
    embed_size = n_dp * width
    embed_rows = both[:embed_size].reshape(n_dp, width)
    grad_b_up = both[embed_size : embed_size + hidden]
    rest = both[embed_size + hidden :].reshape(6, width)
    grad_b_down, grad_gain_two, grad_shift_two, grad_b_out, grad_gain_one, grad_shift_one = (
        rest[r] for r in range(6)
    )

    embeds = lax.dynamic_slice_in_dim(
        jnp.take(time_table, steps_all, axis=0), dp * out_rows, out_rows, axis=1
    ).astype(f32)
    grad_t_query = jnp.dot(embeds.T, image_sums[:, :group], precision=HIGHEST)
    grad_t_value = jnp.dot(embeds.T, image_sums[:, group : 2 * group], precision=HIGHEST)
    onehot = (
        steps_all[:, None] == jnp.arange(table_rows, dtype=jnp.int32)[None, :]
    ).astype(f32)
    grad_time_table = jnp.dot(onehot.T, embed_rows, precision=HIGHEST)

    return (
        result[None],
        grad_tokens[None],
        grad_qkv[:, 0],
        grad_qkv[:, 1],
        grad_qkv[:, 2],
        grad_t_query,
        grad_t_value,
        grad_w_out,
        grad_w_up,
        grad_w_down,
        grad_gain_one,
        grad_shift_one,
        grad_b_query,
        grad_b_value,
        grad_b_out,
        grad_gain_two,
        grad_shift_two,
        grad_b_up,
        grad_b_down,
        grad_bias_table,
        grad_time_table,
    )


def solution(mesh):
    split, copied, by_block = P("dp", "seq", None), P(), P("dp", "seq")
    in_specs = (split, P("dp"), P("seq", None)) + (copied,) * 19 + (split,)
    out_specs = (split, split) + (by_block,) * 8 + (copied,) * 11
    return jax.shard_map(
        per_device, mesh=mesh, in_specs=in_specs, out_specs=out_specs, check_vma=False
    )
```

time: 648 us -> 409 us (0.63)
  waiting for transfers between devices: 229 us -> 45.9 us
  blocking collectives: 88.9 us -> 0 us
  local copies, waits for them, and re-layouts: 134 us -> 64.4 us
  Pallas kernels: 80.4 us -> 145 us
  starting transfers between devices: 18.6 us -> 70.8 us
  matrix products: 47.5 us -> 17.2 us
  other arithmetic: 21.9 us -> 40.8 us
    all_to_all x1 -> x0, blocking collectives: 82.3 us -> none  [per_device(): parts = lax.all_to_all(parts, 'dp', 0, 0)]
    unnamed x12 -> x3, waiting for transfers between devices: 79.3 us -> 0.71 us
    pallas_call x3 -> x12, Pallas kernels: 80.4 us -> 145 us  [the longest x2 31.3 us: attend_back(): pl.pallas_call(partial(attend_back_kernel, head_size, groups), grid=(head...]
    ppermute x0 -> x44, starting transfers between devices: none -> 62 us  [exchange(): return lax.ppermute(array, axis, [(i, i ^ step) for i in range(size)])]
    psum x1 -> x0, waiting for transfers between devices: 48.9 us -> none  [per_device(): vector = lax.psum(jnp.concatenate(apart + summed + images), 'dp')]
    another operation x35 -> x10, local copies, waits for them, and re-layouts: 53.7 us -> 5.87 us  [the longest x9 5.67 us: per_device(): jnp.stack([gain_one, shift_one, b_query, b_value, b_out, gain_two, shift_...]
    ppermute x0 -> x44, waiting for transfers between devices: none -> 45.2 us  [exchange(): return lax.ppermute(array, axis, [(i, i ^ step) for i in range(size)])]
    all_gather x1, waiting for transfers between devices: 34.3 us -> 0.01 us  [per_device(): dy_all = lax.all_gather(dy, 'dp', axis=0)]
  transfers between devices with their start and end apart: 13 -> 49, of which waited for: 9 -> 10; matrix products, arithmetic and copies ran while one was open for 26% -> 26% of each run, Pallas kernels for 0% -> 29%
where the time goes in v2:
time: 409 us; the launch traced here: 401 us
  Pallas kernels  145 us (35%)
  starting transfers between devices  70.8 us (17%)
  local copies, waits for them, and re-layouts  64.4 us (16%)
  waiting for transfers between devices  45.9 us (11%)
  other arithmetic  40.8 us (10%)
  between operations  17.5 us (4%)
  matrix products  17.2 us (4%)
    ppermute x44, starting transfers between devices, exchange(): return lax.ppermute(array, axis, [(i, i ^ step) for i in range(size)])  62 us
    ppermute x44, waiting for transfers between devices, exchange(): return lax.ppermute(array, axis, [(i, i ^ step) for i in range(size)])  45.2 us
    pallas_call x2, Pallas kernels, attend_back(): pl.pallas_call(partial(attend_back_kernel, head_size, groups), grid=(head...  31.3 us
    pallas_call x2, Pallas kernels, attend(): pl.pallas_call(partial(attend_kernel, head_size, groups), grid=(heads,),...  26.9 us
    pallas_call x1, Pallas kernels, mlp_second(): pl.pallas_call(partial(mlp_second_kernel, groups, step), in_specs=[IN_SME...  15.7 us
    pallas_call x1, Pallas kernels, mlp_first(): pl.pallas_call(partial(mlp_first_kernel, len(mixed) // 2, step), in_specs...  15.1 us
    unnamed x110, local copies, waits for them, and re-layouts  13.2 us
    pallas_call x1, Pallas kernels, bias_strips(): pl.pallas_call(strips_kernel, grid=(heads,), in_specs=[per_head(table.sha...  10.9 us
  transfers between devices with their start and end apart: 49, of which 10 were waited for; matrix products, arithmetic and copies ran while one was open for 26% of the time, Pallas kernels for 29%

profile of v2, /device:TPU:0, one launch (start us, length us, event | category | flops | bytes accessed | tf_op | source)
XLA Modules:
  0.0 401.5 jit_solution(10324205621485940167)
XLA Ops:
  15.5 9.4 %project.1 = (bf16[432,256]{1,0:T(8,128)(2,1)}, bf16[432,256]{1,0:T(8,128)(2,1)}, bf16[432,256]{1,0:T(8,128)(2,1)}, bf16[432,256]{1,0:T(8,128)(2,1)}, bf16[432,2...) custom-call(s32[1]{0:T(128)} %bitcast.seq_ref, ...), custom_call_target="tpu_custom_call" | custom-call | flops 1800000000 | bytes 5400000 | tf_op jit(solution)/shard_map/project/pallas_call | solution.py:655
  25.0 3.1 collective-permute-start.3
  28.1 2.6 collective-permute-start.4
  31.6 3.5 collective-permute-start.1
  38.4 3.5 constant_dynamic-slice_fusion.6
  41.9 2.3 copy.101
  53.0 10.9 %strips.1.strips_ref = f32[4,4,32,2048]{3,2,1,0:T(8,128)} custom-call(f32[4,72,128]{2,1,0:T(8,128)} %pad.20.table_ref), custom_call_target="tpu_custom_call" | custom-call | flops 1800000000 | bytes 5400000 | tf_op jit(solution)/shard_map/strips/pallas_call | solution.py:640
  65.4 13.4 %attend.2 = (bf16[144,256]{1,0:T(8,128)(2,1)}, bf16[144,256]{1,0:T(8,128)(2,1)}, bf16[144,256]{1,0:T(8,128)(2,1)}, bf16[144,256]{1,0:T(8,128)(2,1)}, bf16[432,10...) custom-call(s32[1]{0:T(128)} %bitcast.seq_ref, ...), custom_call_target="tpu_custom_call" | custom-call | flops 2600000000 | bytes 7800000 | tf_op jit(solution)/shard_map/attend/pallas_call | solution.py:687
  79.6 13.5 %attend.3 = (bf16[144,256]{1,0:T(8,128)(2,1)}, bf16[144,256]{1,0:T(8,128)(2,1)}, bf16[144,256]{1,0:T(8,128)(2,1)}, bf16[144,256]{1,0:T(8,128)(2,1)}, bf16[432,10...) custom-call(s32[1]{0:T(128)} %bitcast.seq_ref, ...), custom_call_target="tpu_custom_call" | custom-call | flops 2600000000 | bytes 7800000 | tf_op jit(solution)/shard_map/attend/pallas_call | solution.py:687
  94.7 2.3 collective-permute-start.11
  101.0 3.7 collective-permute-start.8
  105.4 2.3 collective-permute-done.7.refs_2_
  108.3 15.1 %mlp_first.1 = (bf16[256,4608]{1,0:T(8,128)(2,1)}, bf16[4608,256]{1,0:T(8,128)(2,1)}, bf16[256,4608]{1,0:T(8,128)(2,1)}, bf16[1152,256]{1,0:T(8,128)(2,1)}, bf16...) custom-call(s32[1]{0:T(128)} %bitcast.seq_ref, bf16[256,1152]{1,0:T(8,128)(2,1)} %bitcast.110, ...), custom_call_target="tpu_custom_call" | custom-call | flops 2800000000 | bytes 8400000 | tf_op jit(solution)/shard_map/mlp_first/pallas_call | solution.py:761
  123.6 4.5 %all-to-all-start = ((bf16[8,576,256]{2,1,0:T(8,128)(2,1)}), bf16[8,576,256]{2,1,0:T(8,128)(2,1)}, u32[]{:S(2)}, u32[]{:S(2)}) async-start(bf16[8,576,256]{2,1,0:T(8,128)(2,1)} %bitcast.121), calls=%async_computation | async-start | bytes 4718592 | tf_op jit(solution)/shard_map/all_to_all | solution.py:1076
  134.7 9.1 %up_grad.1 = (bf16[2,288,1152]{2,1,0:T(8,128)(2,1)}, bf16[2,288,1152]{2,1,0:T(8,128)(2,1)}, bf16[2,288,1152]{2,1,0:T(8,128)(2,1)}, bf16[2,288,1152]{2,1,0:T(8,128)(2,1)}) custom-call(s32[4]{0:T(128)} %iota_xor_fusion.order_ref, bf16[2,576,256]{2,1,0:T(8,128)(2,1)} %bitcast.125, bf16[2,576,256]{2,1,0:T(8,128)(2,1)} %collective-permute-done.12.other_ref, ...), custom_call_target="tpu_custom_call" | custom-call | flops 1600000000 | bytes 4800000 | tf_op jit(solution)/shard_map/up_grad/pallas_call | solution.py:837
  147.0 15.7 %mlp_second.1 = (bf16[144,256]{1,0:T(8,128)(2,1)}, bf16[144,256]{1,0:T(8,128)(2,1)}, bf16[144,256]{1,0:T(8,128)(2,1)}, bf16[144,256]{1,0:T(8,128)(2,1)}, bf16[14...) custom-call(s32[1]{0:T(128)} %bitcast.seq_ref, ...), custom_call_target="tpu_custom_call" | custom-call | flops 2800000000 | bytes 8400000 | tf_op jit(solution)/shard_map/mlp_second/pallas_call | solution.py:798
  164.1 2.4 collective-permute-start.15
  171.9 10.3 %down_grad.1 = bf16[1152,576]{1,0:T(8,128)(2,1)} custom-call(bf16[8,576,256]{2,1,0:T(8,128)(2,1)} %all-to-all-done.act_ref, bf16[8,256,1152]{2,1,0:T(8,128)(2,1)} %all-gather.4.cloned.1.call-done.dy_ref), custom_call_target="tpu_custom_call" | custom-call | flops 1600000000 | bytes 4800000 | tf_op jit(solution)/shard_map/down_grad/pallas_call | solution.py:855
  182.8 3.4 collective-permute-start.18
  186.9 15.7 %attend_back.2 = (bf16[432,256]{1,0:T(8,128)(2,1)}, bf16[432,256]{1,0:T(8,128)(2,1)}, bf16[432,256]{1,0:T(8,128)(2,1)}, bf16[432,256]{1,0:T(8,128)(2,1)}, f32[2,4,32,2048]{3,2,1,0:T(8,128)}) custom-call(s32[1]{0:T(128)} %bitcast.seq_ref, bf16[432,1024]{1,0:T(8,128)(2,1)} %get-tuple-element.175.qkv_ref, bf16[2,1024,1024]{2,1,0:T(8,128)(2,1)} %get-tuple-element.176.expo_ref, ...), custom_call_target="tpu_custom_call" | custom-call | flops 3200000000 | bytes 9600000 | tf_op jit(solution)/shard_map/attend_back/pallas_call | solution.py:720
  202.8 3.7 collective-permute-start.21
  206.6 3.2 constant_dynamic-update-slice_fusion.1
  210.6 2.7 add_convert_fusion
  213.2 2.7 add_convert_fusion.2
  216.5 15.6 %attend_back.3 = (bf16[432,256]{1,0:T(8,128)(2,1)}, bf16[432,256]{1,0:T(8,128)(2,1)}, bf16[432,256]{1,0:T(8,128)(2,1)}, bf16[432,256]{1,0:T(8,128)(2,1)}, f32[2,4,32,2048]{3,2,1,0:T(8,128)}) custom-call(s32[1]{0:T(128)} %bitcast.seq_ref, bf16[432,1024]{1,0:T(8,128)(2,1)} %get-tuple-element.201.qkv_ref, bf16[2,1024,1024]{2,1,0:T(8,128)(2,1)} %get-tuple-element.202.expo_ref, ...), custom_call_target="tpu_custom_call" | custom-call | flops 3200000000 | bytes 9600000 | tf_op jit(solution)/shard_map/attend_back/pallas_call | solution.py:720
  232.1 3.1 constant_dynamic-update-slice_fusion
  235.2 2.4 slice_bitcast_fusion.3
  238.6 3.2 reshape.207
  241.8 4.2 %convolution_bitcast_fusion = f32[4,63,63]{2,1,0:T(8,128)S(1)} fusion(f32[4,32,63,32]{3,2,1,0:T(8,128)} %reshape.207, s32[32,32]{1,0:T(8,128)S(1)} %iota_add_fusion), kind=kOutput, calls=%fused_computation.20 | convolution fusion | flops 195148800 | bytes 1099792 | tf_op jit(solution)/shard_map/hjai,jib->hab/dot_general | solution.py:981
  248.5 3.8 collective-permute-start.26
  253.4 2.9 collective-permute-done.25.refs_5_
  256.8 11.2 %collective-permute-done.26.refs_6_ = bf16[432,256]{1,0:T(8,128)(2,1)S(1)} collective-permute-done((bf16[432,256]{1,0:T(8,128)(2,1)}, bf16[432,256]{1,0:T(8,128)(2,1)S(1)}, u32[]{:S(2)}, u32[]{:S(2)}) %collective-permute-start.26) | collective-permute-done | bytes 221216 | tf_op jit(solution)/shard_map/ppermute | solution.py:905
  268.7 9.0 %token_grad.1 = bf16[256,1152]{1,0:T(8,128)(2,1)} custom-call(s32[1]{0:T(128)} %bitcast.seq_ref, bf16[256,1152]{1,0:T(8,128)(2,1)} %bitcast.111, f32[256,1152]{1,0:T(8,128)} %get-tuple-element.174.middle_ref, f32[8,1,1152]{2,1,0:T(1,128)} %broadcast_in_dim.87.rows_ref, bf16[1152,1152]{1,0:T(8,128)(2,1)} %wq_hbm.3, bf16[1152,1152]{1,0:T(8,128)(2,1)} %wk_hbm.3, ...), custom_call_target="tpu_custom_call" | custom-call | flops 1800000000 | bytes 5400000 | tf_op jit(solution)/shard_map/token_grad/pallas_call | solution.py:887
  277.8 2.2 add_convert_fusion.6
  281.0 7.2 %qkv_grad.1 = (bf16[2,1152,432]{2,1,0:T(8,128)(2,1)}, f32[864,1]{1,0:T(8,128)}, f32[8,1152]{1,0:T(8,128)}) custom-call(s32[1]{0:T(128)} %bitcast.seq_ref, bf16[4,256,1152]{2,1,0:T(8,128)(2,1)} %bitcast.129, bf16[864,1152]{1,0:T(8,128)(2,1)} %bitcast.122, f32[8,1,1152]{2,1,0:T(1,128)} %broadcast_in_dim.87.rows_ref, ...), custom_call_target="tpu_custom_call" | custom-call | flops 1800000000 | bytes 5400000 | tf_op jit(solution)/shard_map/qkv_grad/pallas_call | solution.py:870
  290.1 2.2 convolution_reduce_fusion
  292.4 2.2 convolution_reduce_fusion.1
  296.2 4.0 collective-permute-start.40
  306.3 2.8 collective-permute-done.40
  309.9 3.0 collective-permute-start.41
  312.8 2.7 collective-permute-done.34
  317.4 2.1 reshape.213
  321.3 4.1 %all-to-all-start.1 = ((bf16[4,144,288]{2,1,0:T(8,128)(2,1)}), bf16[4,144,288]{2,1,0:T(8,128)(2,1)}, u32[]{:S(2)}, u32[]{:S(2)}) async-start(bf16[4,144,288]{2,1,0:T(8,128)(2,1)} %copy.97), calls=%async_computation.1 | async-start | bytes 884736 | tf_op jit(solution)/shard_map/all_to_all | solution.py:1117
  334.1 4.3 %collective-permute-done.42 = f32[1,37188]{1,0:T(1,128)} collective-permute-done((f32[1,37188]{1,0:T(1,128)}, f32[1,37188]{1,0:T(1,128)}, u32[]{:S(2)}, u32[]{:S(2)}) %collective-permute-start.42) | collective-permute-done | bytes 148784 | tf_op jit(solution)/shard_map/ppermute | solution.py:905
  348.1 7.4 %collective-permute-done.43 = f32[2,37188]{1,0:T(2,128)} collective-permute-done((f32[2,37188]{1,0:T(2,128)}, f32[2,37188]{1,0:T(2,128)}, u32[]{:S(2)}, u32[]{:S(2)}) %collective-permute-start.43) | collective-permute-done | bytes 297536 | tf_op jit(solution)/shard_map/ppermute | solution.py:905
  363.8 4.4 %fusion.12 = f32[1000,1152]{1,0:T(8,128)} fusion(f32[8,1152]{1,0:T(8,128)S(1)} %slice.209, s32[8]{0:T(128)S(1)} %get-tuple-element.246), kind=kOutput, calls=%fused_computation.66 | convolution fusion | flops 110600000 | bytes 4644896 | tf_op jit(solution)/shard_map/dot_general | solution.py:1167
  368.2 8.1 %collective-permute-done.31 = bf16[2,2,144,432]{3,2,1,0:T(8,128)(2,1)} collective-permute-done((bf16[2,2,144,432]{3,2,1,0:T(8,128)(2,1)S(1)}, bf16[2,2,144,432]{3,2,1,0:T(8,128)(2,1)}, u32[]{:S(2)}, u32[]{:S(2)}) %collective-permute-start.31) | collective-permute-done | bytes 497696 | tf_op jit(solution)/shard_map/ppermute | solution.py:905
  384.3 2.4 collective-permute-done.32
  (290 shorter events, 110.4 us)
Async XLA Ops:
  7.2 58.1 %all-gather.4.cloned.1.call-start = ((), (), s32[]{:S(2)}) async-start(), calls=%async_computation.3 | async-start | bytes 5308416 | tf_op jit(solution)/shard_map/all_gather | solution.py:1037
  7.9 273.1 %all-gather.6.cloned.1.call-start = ((), (), s32[]{:S(2)}) async-start(), calls=%async_computation.5 | async-start | bytes 2949120 | tf_op jit(solution)/shard_map/all_gather | solution.py:1051
  25.0 40.3 %collective-permute-start.3 = (bf16[432,256]{1,0:T(8,128)(2,1)}, bf16[432,256]{1,0:T(8,128)(2,1)}, u32[]{:S(2)}, u32[]{:S(2)}) collective-permute-start(bf16[432,256]{1,0:T(8,128)(2,1)} %get-tuple-element.143), channel_id=1, source_target_pairs={{0,1},{1,0},{2,3},{3,2},{4,5},{5,4},{6,7},{7,6},{8,9},{9,8},{10,11... | collective-permute-start | bytes 663560 | tf_op jit(solution)/shard_map/ppermute | solution.py:905
  28.1 37.3 %collective-permute-start.4 = (bf16[432,256]{1,0:T(8,128)(2,1)}, bf16[432,256]{1,0:T(8,128)(2,1)}, u32[]{:S(2)}, u32[]{:S(2)}) collective-permute-start(bf16[432,256]{1,0:T(8,128)(2,1)} %get-tuple-element.144), channel_id=1, source_target_pairs={{0,2},{1,3},{2,0},{3,1},{4,6},{5,7},{6,4},{7,5},{8,10},{9,11},{10,... | collective-permute-start | bytes 663560 | tf_op jit(solution)/shard_map/ppermute | solution.py:905
  30.7 34.7 %collective-permute-start.5 = (bf16[432,256]{1,0:T(8,128)(2,1)}, bf16[432,256]{1,0:T(8,128)(2,1)}, u32[]{:S(2)}, u32[]{:S(2)}) collective-permute-start(bf16[432,256]{1,0:T(8,128)(2,1)} %get-tuple-element.145), channel_id=1, source_target_pairs={{0,3},{1,2},{2,1},{3,0},{4,7},{5,6},{6,5},{7,4},{8,11},{9,10},{10,... | collective-permute-start | bytes 663560 | tf_op jit(solution)/shard_map/ppermute | solution.py:905
  30.7 48.1 %collective-permute-start = (bf16[432,256]{1,0:T(8,128)(2,1)}, bf16[432,256]{1,0:T(8,128)(2,1)S(1)}, u32[]{:S(2)}, u32[]{:S(2)}) collective-permute-start(bf16[432,256]{1,0:T(8,128)(2,1)} %get-tuple-element.135), channel_id=1, source_target_pairs={{0,1},{1,0},{2,3},{3,2},{4,5},{5,4},{6,7},{7,6},{8,9},{9,8},{10,11... | collective-permute-start | bytes 663560 | tf_op jit(solution)/shard_map/ppermute | solution.py:905
  31.6 47.3 %collective-permute-start.1 = (bf16[432,256]{1,0:T(8,128)(2,1)}, bf16[432,256]{1,0:T(8,128)(2,1)}, u32[]{:S(2)}, u32[]{:S(2)}) collective-permute-start(bf16[432,256]{1,0:T(8,128)(2,1)} %get-tuple-element.136), channel_id=1, source_target_pairs={{0,2},{1,3},{2,0},{3,1},{4,6},{5,7},{6,4},{7,5},{8,10},{9,11},{10,... | collective-permute-start | bytes 663560 | tf_op jit(solution)/shard_map/ppermute | solution.py:905
  65.3 13.5 %collective-permute-start.2 = (bf16[432,256]{1,0:T(8,128)(2,1)S(1)}, bf16[432,256]{1,0:T(8,128)(2,1)S(1)}, u32[]{:S(2)}, u32[]{:S(2)}) collective-permute-start(bf16[432,256]{1,0:T(8,128)(2,1)S(1)} %copy-done.37), channel_id=1, source_target_pairs={{0,3},{1,2},{2,1},{3,0},{4,7},{5,6},{6,5},{7,4},{8,11},{9,10},{10,... | collective-permute-start | bytes 663560 | tf_op jit(solution)/shard_map/ppermute | solution.py:905
  93.1 7.9 %collective-permute-start.10 = (bf16[144,256]{1,0:T(8,128)(2,1)}, bf16[144,256]{1,0:T(8,128)(2,1)S(1)}, u32[]{:S(2)}, u32[]{:S(2)}) collective-permute-start(bf16[144,256]{1,0:T(8,128)(2,1)} %get-tuple-element.161), channel_id=1, source_target_pairs={{0,2},{1,3},{2,0},{3,1},{4,6},{5,7},{6,4},{7,5},{8,10},{9,11},{10,... | collective-permute-start | bytes 221192 | tf_op jit(solution)/shard_map/ppermute | solution.py:905
  94.7 10.6 %collective-permute-start.11 = (bf16[144,256]{1,0:T(8,128)(2,1)}, bf16[144,256]{1,0:T(8,128)(2,1)S(1)}, u32[]{:S(2)}, u32[]{:S(2)}) collective-permute-start(bf16[144,256]{1,0:T(8,128)(2,1)} %get-tuple-element.162), channel_id=1, source_target_pairs={{0,3},{1,2},{2,1},{3,0},{4,7},{5,6},{6,5},{7,4},{8,11},{9,10},{10,... | collective-permute-start | bytes 221192 | tf_op jit(solution)/shard_map/ppermute | solution.py:905
  97.0 8.3 %collective-permute-start.9 = (bf16[144,256]{1,0:T(8,128)(2,1)}, bf16[144,256]{1,0:T(8,128)(2,1)S(1)}, u32[]{:S(2)}, u32[]{:S(2)}) collective-permute-start(bf16[144,256]{1,0:T(8,128)(2,1)} %get-tuple-element.160), channel_id=1, source_target_pairs={{0,1},{1,0},{2,3},{3,2},{4,5},{5,4},{6,7},{7,6},{8,9},{9,8},{10,11... | collective-permute-start | bytes 221192 | tf_op jit(solution)/shard_map/ppermute | solution.py:905
  97.5 7.8 %collective-permute-start.6 = (bf16[144,256]{1,0:T(8,128)(2,1)S(1)}, bf16[144,256]{1,0:T(8,128)(2,1)S(1)}, u32[]{:S(2)}, u32[]{:S(2)}) collective-permute-start(bf16[144,256]{1,0:T(8,128)(2,1)S(1)} %copy-done.49), channel_id=1, source_target_pairs={{0,1},{1,0},{2,3},{3,2},{4,5},{5,4},{6,7},{7,6},{8,9},{9,8},{10,11... | collective-permute-start | bytes 221192 | tf_op jit(solution)/shard_map/ppermute | solution.py:905
  99.0 8.6 %collective-permute-start.7 = (bf16[144,256]{1,0:T(8,128)(2,1)S(1)}, bf16[144,256]{1,0:T(8,128)(2,1)S(1)}, u32[]{:S(2)}, u32[]{:S(2)}) collective-permute-start(bf16[144,256]{1,0:T(8,128)(2,1)S(1)} %copy-done.47), channel_id=1, source_target_pairs={{0,2},{1,3},{2,0},{3,1},{4,6},{5,7},{6,4},{7,5},{8,10},{9,11},{10,... | collective-permute-start | bytes 221192 | tf_op jit(solution)/shard_map/ppermute | solution.py:905
  101.0 6.6 %collective-permute-start.8 = (bf16[144,256]{1,0:T(8,128)(2,1)S(1)}, bf16[144,256]{1,0:T(8,128)(2,1)S(1)}, u32[]{:S(2)}, u32[]{:S(2)}) collective-permute-start(bf16[144,256]{1,0:T(8,128)(2,1)S(1)} %copy-done.46), channel_id=1, source_target_pairs={{0,3},{1,2},{2,1},{3,0},{4,7},{5,6},{6,5},{7,4},{8,11},{9,10},{10,... | collective-permute-start | bytes 221192 | tf_op jit(solution)/shard_map/ppermute | solution.py:905
  123.4 11.3 %collective-permute-start.13 = (bf16[256,4608]{1,0:T(8,128)(2,1)}, bf16[256,4608]{1,0:T(8,128)(2,1)}, u32[]{:S(2)}, u32[]{:S(2)}) collective-permute-start(bf16[256,4608]{1,0:T(8,128)(2,1)} %get-tuple-element.166.inner_ref), channel_id=1, source_target_pairs={{0,4},{4,0},{8,12},{12,8},{16,20},{20,16},{24,28},{28,24},{1,5},{5... | collective-permute-start | bytes 7077896 | tf_op jit(solution)/shard_map/ppermute | solution.py:905
  123.6 48.3 %all-to-all-start = ((bf16[8,576,256]{2,1,0:T(8,128)(2,1)}), bf16[8,576,256]{2,1,0:T(8,128)(2,1)}, u32[]{:S(2)}, u32[]{:S(2)}) async-start(bf16[8,576,256]{2,1,0:T(8,128)(2,1)} %bitcast.121), calls=%async_computation | async-start | bytes 4718592 | tf_op jit(solution)/shard_map/all_to_all | solution.py:1076
  128.2 216.2 %reduce-scatter.2.cloned.1.call-start = ((), (), s32[]{:S(2)}) async-start(), calls=%async_computation.4 | async-start | bytes 1843200 | tf_op jit(solution)/shard_map/reduce_scatter | solution.py:1085
  143.7 66.1 %collective-permute-start.24 = (bf16[2,288,1152]{2,1,0:T(8,128)(2,1)}, bf16[2,288,1152]{2,1,0:T(8,128)(2,1)}, u32[]{:S(2)}, u32[]{:S(2)}) collective-permute-start(bf16[2,288,1152]{2,1,0:T(8,128)(2,1)} %get-tuple-element.208), channel_id=1, source_target_pairs={{0,16},{4,20},{8,24},{12,28},{16,0},{20,4},{24,8},{28,12},{1,17},{... | collective-permute-start | bytes 3981320 | tf_op jit(solution)/shard_map/ppermute | solution.py:905
  145.5 67.7 %collective-permute-start.23 = (bf16[2,288,1152]{2,1,0:T(8,128)(2,1)}, bf16[2,288,1152]{2,1,0:T(8,128)(2,1)}, u32[]{:S(2)}, u32[]{:S(2)}) collective-permute-start(bf16[2,288,1152]{2,1,0:T(8,128)(2,1)} %get-tuple-element.206), channel_id=1, source_target_pairs={{0,8},{4,12},{8,0},{12,4},{16,24},{20,28},{24,16},{28,20},{1,9},{5... | collective-permute-start | bytes 3981320 | tf_op jit(solution)/shard_map/ppermute | solution.py:905
  162.7 19.6 %collective-permute-start.14 = (bf16[144,256]{1,0:T(8,128)(2,1)}, bf16[144,256]{1,0:T(8,128)(2,1)S(1)}, u32[]{:S(2)}, u32[]{:S(2)}) collective-permute-start(bf16[144,256]{1,0:T(8,128)(2,1)} %get-tuple-element.182), channel_id=1, source_target_pairs={{0,1},{1,0},{2,3},{3,2},{4,5},{5,4},{6,7},{7,6},{8,9},{9,8},{10,11... | collective-permute-start | bytes 221192 | tf_op jit(solution)/shard_map/ppermute | solution.py:905
  164.1 18.7 %collective-permute-start.15 = (bf16[144,256]{1,0:T(8,128)(2,1)}, bf16[144,256]{1,0:T(8,128)(2,1)S(1)}, u32[]{:S(2)}, u32[]{:S(2)}) collective-permute-start(bf16[144,256]{1,0:T(8,128)(2,1)} %get-tuple-element.183), channel_id=1, source_target_pairs={{0,2},{1,3},{2,0},{3,1},{4,6},{5,7},{6,4},{7,5},{8,10},{9,11},{10,... | collective-permute-start | bytes 221192 | tf_op jit(solution)/shard_map/ppermute | solution.py:905
  166.5 19.7 %collective-permute-start.16 = (bf16[144,256]{1,0:T(8,128)(2,1)}, bf16[144,256]{1,0:T(8,128)(2,1)S(1)}, u32[]{:S(2)}, u32[]{:S(2)}) collective-permute-start(bf16[144,256]{1,0:T(8,128)(2,1)} %get-tuple-element.184), channel_id=1, source_target_pairs={{0,3},{1,2},{2,1},{3,0},{4,7},{5,6},{6,5},{7,4},{8,11},{9,10},{10,... | collective-permute-start | bytes 221192 | tf_op jit(solution)/shard_map/ppermute | solution.py:905
  182.3 20.3 %collective-permute-start.17 = (bf16[144,256]{1,0:T(8,128)(2,1)S(1)}, bf16[144,256]{1,0:T(8,128)(2,1)S(1)}, u32[]{:S(2)}, u32[]{:S(2)}) collective-permute-start(bf16[144,256]{1,0:T(8,128)(2,1)S(1)} %copy-done.48), channel_id=1, source_target_pairs={{0,1},{1,0},{2,3},{3,2},{4,5},{5,4},{6,7},{7,6},{8,9},{9,8},{10,11... | collective-permute-start | bytes 221192 | tf_op jit(solution)/shard_map/ppermute | solution.py:905
  182.8 19.9 %collective-permute-start.18 = (bf16[144,256]{1,0:T(8,128)(2,1)S(1)}, bf16[144,256]{1,0:T(8,128)(2,1)S(1)}, u32[]{:S(2)}, u32[]{:S(2)}) collective-permute-start(bf16[144,256]{1,0:T(8,128)(2,1)S(1)} %copy-done.45), channel_id=1, source_target_pairs={{0,2},{1,3},{2,0},{3,1},{4,6},{5,7},{6,4},{7,5},{8,10},{9,11},{10,... | collective-permute-start | bytes 221192 | tf_op jit(solution)/shard_map/ppermute | solution.py:905
  186.2 16.5 %collective-permute-start.19 = (bf16[144,256]{1,0:T(8,128)(2,1)S(1)}, bf16[144,256]{1,0:T(8,128)(2,1)S(1)}, u32[]{:S(2)}, u32[]{:S(2)}) collective-permute-start(bf16[144,256]{1,0:T(8,128)(2,1)S(1)} %copy-done.44), channel_id=1, source_target_pairs={{0,3},{1,2},{2,1},{3,0},{4,7},{5,6},{6,5},{7,4},{8,11},{9,10},{10,... | collective-permute-start | bytes 221192 | tf_op jit(solution)/shard_map/ppermute | solution.py:905
  202.6 43.6 %collective-permute-start.36 = (bf16[2,2,144,1152]{3,2,1,0:T(8,128)(2,1)}, bf16[2,2,144,1152]{3,2,1,0:T(8,128)(2,1)}, u32[]{:S(2)}, u32[]{:S(2)}) collective-permute-start(bf16[2,2,144,1152]{3,2,1,0:T(8,128)(2,1)} %dynamic-slice_bitcast_fusion), channel_id=1, source_target_pairs={{0,4},{4,0},{8,12},{12,8},{16,20},{20,16},{24,28},{28,24},{1,5},{5... | collective-permute-start | bytes 3981320 | tf_op jit(solution)/shard_map/ppermute | solution.py:905
  202.7 45.7 %collective-permute-start.20 = (bf16[432,256]{1,0:T(8,128)(2,1)}, bf16[432,256]{1,0:T(8,128)(2,1)}, u32[]{:S(2)}, u32[]{:S(2)}) collective-permute-start(bf16[432,256]{1,0:T(8,128)(2,1)} %get-tuple-element.198.refs_1_), channel_id=1, source_target_pairs={{0,1},{1,0},{2,3},{3,2},{4,5},{5,4},{6,7},{7,6},{8,9},{9,8},{10,11... | collective-permute-start | bytes 663560 | tf_op jit(solution)/shard_map/ppermute | solution.py:905
  202.8 49.5 %collective-permute-start.21 = (bf16[432,256]{1,0:T(8,128)(2,1)}, bf16[432,256]{1,0:T(8,128)(2,1)}, u32[]{:S(2)}, u32[]{:S(2)}) collective-permute-start(bf16[432,256]{1,0:T(8,128)(2,1)} %get-tuple-element.199.refs_2_), channel_id=1, source_target_pairs={{0,2},{1,3},{2,0},{3,1},{4,6},{5,7},{6,4},{7,5},{8,10},{9,11},{10,... | collective-permute-start | bytes 663560 | tf_op jit(solution)/shard_map/ppermute | solution.py:905
  209.9 43.1 %collective-permute-start.22 = (bf16[432,256]{1,0:T(8,128)(2,1)}, bf16[432,256]{1,0:T(8,128)(2,1)}, u32[]{:S(2)}, u32[]{:S(2)}) collective-permute-start(bf16[432,256]{1,0:T(8,128)(2,1)} %get-tuple-element.200.refs_3_), channel_id=1, source_target_pairs={{0,3},{1,2},{2,1},{3,0},{4,7},{5,6},{6,5},{7,4},{8,11},{9,10},{10,... | collective-permute-start | bytes 663560 | tf_op jit(solution)/shard_map/ppermute | solution.py:905
  215.9 61.8 %collective-permute-start.29 = (bf16[2,144,1152]{2,1,0:T(8,128)(2,1)}, bf16[2,144,1152]{2,1,0:T(8,128)(2,1)}, u32[]{:S(2)}, u32[]{:S(2)}) collective-permute-start(bf16[2,144,1152]{2,1,0:T(8,128)(2,1)} %get-tuple-element.225), channel_id=1, source_target_pairs={{0,8},{4,12},{8,0},{12,4},{16,24},{20,28},{24,16},{28,20},{1,9},{5... | collective-permute-start | bytes 1990664 | tf_op jit(solution)/shard_map/ppermute | solution.py:905
  246.2 10.0 %collective-permute-start.25 = (bf16[432,256]{1,0:T(8,128)(2,1)S(1)}, bf16[432,256]{1,0:T(8,128)(2,1)S(1)}, u32[]{:S(2)}, u32[]{:S(2)}) collective-permute-start(bf16[432,256]{1,0:T(8,128)(2,1)S(1)} %copy-done.39), channel_id=1, source_target_pairs={{0,1},{1,0},{2,3},{3,2},{4,5},{5,4},{6,7},{7,6},{8,9},{9,8},{10,11... | collective-permute-start | bytes 663560 | tf_op jit(solution)/shard_map/ppermute | solution.py:905
  248.5 19.5 %collective-permute-start.26 = (bf16[432,256]{1,0:T(8,128)(2,1)}, bf16[432,256]{1,0:T(8,128)(2,1)S(1)}, u32[]{:S(2)}, u32[]{:S(2)}) collective-permute-start(bf16[432,256]{1,0:T(8,128)(2,1)} %get-tuple-element.230.refs_6_), channel_id=1, source_target_pairs={{0,2},{1,3},{2,0},{3,1},{4,6},{5,7},{6,4},{7,5},{8,10},{9,11},{10,... | collective-permute-start | bytes 663560 | tf_op jit(solution)/shard_map/ppermute | solution.py:905
  252.3 15.7 %collective-permute-start.27 = (bf16[432,256]{1,0:T(8,128)(2,1)}, bf16[432,256]{1,0:T(8,128)(2,1)S(1)}, u32[]{:S(2)}, u32[]{:S(2)}) collective-permute-start(bf16[432,256]{1,0:T(8,128)(2,1)} %get-tuple-element.231.refs_7_), channel_id=1, source_target_pairs={{0,3},{1,2},{2,1},{3,0},{4,7},{5,6},{6,5},{7,4},{8,11},{9,10},{10,... | collective-permute-start | bytes 663560 | tf_op jit(solution)/shard_map/ppermute | solution.py:905
  252.9 27.1 %collective-permute-start.28 = (bf16[2,144,1152]{2,1,0:T(8,128)(2,1)S(1)}, bf16[2,144,1152]{2,1,0:T(8,128)(2,1)S(1)}, u32[]{:S(2)}, u32[]{:S(2)}) collective-permute-start(bf16[2,144,1152]{2,1,0:T(8,128)(2,1)S(1)} %copy-done.20), channel_id=1, source_target_pairs={{0,16},{4,20},{8,24},{12,28},{16,0},{20,4},{24,8},{28,12},{1,17},{... | collective-permute-start | bytes 1990664 | tf_op jit(solution)/shard_map/ppermute | solution.py:905
  256.3 44.0 %collective-permute-start.37 = (bf16[2,144,1152]{2,1,0:T(8,128)(2,1)S(1)}, bf16[2,144,1152]{2,1,0:T(8,128)(2,1)}, u32[]{:S(2)}, u32[]{:S(2)}) collective-permute-start(bf16[2,144,1152]{2,1,0:T(8,128)(2,1)S(1)} %dynamic-slice_bitcast_fusion.2), channel_id=1, source_target_pairs={{0,16},{4,20},{8,24},{12,28},{16,0},{20,4},{24,8},{28,12},{1,17},{... | collective-permute-start | bytes 1990664 | tf_op jit(solution)/shard_map/ppermute | solution.py:905
  296.2 8.4 %collective-permute-start.33 = (f32[41804]{0:T(1024)}, f32[41804]{0:T(1024)S(1)}, u32[]{:S(2)}, u32[]{:S(2)}) collective-permute-start(f32[41804]{0:T(1024)} %concatenate.25), channel_id=1, source_target_pairs={{0,4},{4,0},{8,12},{12,8},{16,20},{20,16},{24,28},{28,24},{1,5},{5... | collective-permute-start | bytes 501656 | tf_op jit(solution)/shard_map/ppermute | solution.py:905
  296.2 12.8 %collective-permute-start.40 = (bf16[1,144,1152]{2,1,0:T(8,128)(2,1)}, bf16[1,144,1152]{2,1,0:T(8,128)(2,1)S(1)}, u32[]{:S(2)}, u32[]{:S(2)}) collective-permute-start(bf16[1,144,1152]{2,1,0:T(8,128)(2,1)} %get-tuple-element.244), channel_id=1, source_target_pairs={{0,1},{1,0},{2,3},{3,2},{4,5},{5,4},{6,7},{7,6},{8,9},{9,8},{10,11... | collective-permute-start | bytes 995336 | tf_op jit(solution)/shard_map/ppermute | solution.py:905
  300.2 42.1 %collective-permute-start.39 = (bf16[1,144,1152]{2,1,0:T(8,128)(2,1)}, bf16[1,144,1152]{2,1,0:T(8,128)(2,1)}, u32[]{:S(2)}, u32[]{:S(2)}) collective-permute-start(bf16[1,144,1152]{2,1,0:T(8,128)(2,1)} %get-tuple-element.242), channel_id=1, source_target_pairs={{0,1},{1,0},{2,3},{3,2},{4,5},{5,4},{6,7},{7,6},{8,9},{9,8},{10,11... | collective-permute-start | bytes 995336 | tf_op jit(solution)/shard_map/ppermute | solution.py:905
  301.8 14.8 %collective-permute-start.38 = (bf16[144,1152]{1,0:T(8,128)(2,1)S(1)}, bf16[144,1152]{1,0:T(8,128)(2,1)S(1)}, u32[]{:S(2)}, u32[]{:S(2)}) collective-permute-start(bf16[144,1152]{1,0:T(8,128)(2,1)S(1)} %dynamic-slice_bitcast_fusion.4), channel_id=1, source_target_pairs={{0,8},{4,12},{8,0},{12,4},{16,24},{20,28},{24,16},{28,20},{1,9},{5... | collective-permute-start | bytes 995336 | tf_op jit(solution)/shard_map/ppermute | solution.py:905
  304.6 53.5 %collective-permute-start.30 = (bf16[2,2,2,144,432]{4,3,2,1,0:T(8,128)(2,1)}, bf16[2,2,2,144,432]{4,3,2,1,0:T(8,128)(2,1)}, u32[]{:S(2)}, u32[]{:S(2)}) collective-permute-start(bf16[2,2,2,144,432]{4,3,2,1,0:T(8,128)(2,1)} %get-tuple-element.258), channel_id=1, source_target_pairs={{0,4},{4,0},{8,12},{12,8},{16,20},{20,16},{24,28},{28,24},{1,5},{5... | collective-permute-start | bytes 2985992 | tf_op jit(solution)/shard_map/ppermute | solution.py:905
  305.6 10.0 %collective-permute-start.34 = (f32[41804]{0:T(1024)S(1)}, f32[41804]{0:T(1024)S(1)}, u32[]{:S(2)}, u32[]{:S(2)}) collective-permute-start(f32[41804]{0:T(1024)S(1)} %add.235), channel_id=1, source_target_pairs={{0,8},{4,12},{8,0},{12,4},{16,24},{20,28},{24,16},{28,20},{1,9},{5... | collective-permute-start | bytes 501656 | tf_op jit(solution)/shard_map/ppermute | solution.py:905
  309.9 32.4 %collective-permute-start.41 = (bf16[1,144,1152]{2,1,0:T(8,128)(2,1)}, bf16[1,144,1152]{2,1,0:T(8,128)(2,1)}, u32[]{:S(2)}, u32[]{:S(2)}) collective-permute-start(bf16[1,144,1152]{2,1,0:T(8,128)(2,1)} %add_convert_fusion.4), channel_id=1, source_target_pairs={{0,2},{1,3},{2,0},{3,1},{4,6},{5,7},{6,4},{7,5},{8,10},{9,11},{10,... | collective-permute-start | bytes 995336 | tf_op jit(solution)/shard_map/ppermute | solution.py:905
  316.2 9.3 %collective-permute-start.35 = (f32[41804]{0:T(1024)}, f32[41804]{0:T(1024)}, u32[]{:S(2)}, u32[]{:S(2)}) collective-permute-start(f32[41804]{0:T(1024)} %add.236), channel_id=1, source_target_pairs={{0,16},{4,20},{8,24},{12,28},{16,0},{20,4},{24,8},{28,12},{1,17},{... | collective-permute-start | bytes 501656 | tf_op jit(solution)/shard_map/ppermute | solution.py:905
  321.3 25.0 %all-to-all-start.1 = ((bf16[4,144,288]{2,1,0:T(8,128)(2,1)}), bf16[4,144,288]{2,1,0:T(8,128)(2,1)}, u32[]{:S(2)}, u32[]{:S(2)}) async-start(bf16[4,144,288]{2,1,0:T(8,128)(2,1)} %copy.97), calls=%async_computation.1 | async-start | bytes 884736 | tf_op jit(solution)/shard_map/all_to_all | solution.py:1117
  329.4 9.0 %collective-permute-start.42 = (f32[1,37188]{1,0:T(1,128)}, f32[1,37188]{1,0:T(1,128)}, u32[]{:S(2)}, u32[]{:S(2)}) collective-permute-start(f32[1,37188]{1,0:T(1,128)} %broadcast_in_dim.99), channel_id=1, source_target_pairs={{0,1},{1,0},{2,3},{3,2},{4,5},{5,4},{6,7},{7,6},{8,9},{9,8},{10,11... | collective-permute-start | bytes 446264 | tf_op jit(solution)/shard_map/ppermute | solution.py:905
  340.4 15.0 %collective-permute-start.43 = (f32[2,37188]{1,0:T(2,128)}, f32[2,37188]{1,0:T(2,128)}, u32[]{:S(2)}, u32[]{:S(2)}) collective-permute-start(f32[2,37188]{1,0:T(2,128)} %pad_maximum_fusion.3), channel_id=1, source_target_pairs={{0,2},{1,3},{2,0},{3,1},{4,6},{5,7},{6,4},{7,5},{8,10},{9,11},{10,... | collective-permute-start | bytes 892520 | tf_op jit(solution)/shard_map/ppermute | solution.py:905
  360.8 15.4 %collective-permute-start.31 = (bf16[2,2,144,432]{3,2,1,0:T(8,128)(2,1)S(1)}, bf16[2,2,144,432]{3,2,1,0:T(8,128)(2,1)}, u32[]{:S(2)}, u32[]{:S(2)}) collective-permute-start(bf16[2,2,144,432]{3,2,1,0:T(8,128)(2,1)S(1)} %dynamic-slice_bitcast_fusion.3), channel_id=1, source_target_pairs={{0,8},{4,12},{8,0},{12,4},{16,24},{20,28},{24,16},{28,20},{1,9},{5... | collective-permute-start | bytes 1493000 | tf_op jit(solution)/shard_map/ppermute | solution.py:905
  378.3 8.4 %collective-permute-start.32 = (bf16[2,144,432]{2,1,0:T(8,128)(2,1)}, bf16[2,144,432]{2,1,0:T(8,128)(2,1)}, u32[]{:S(2)}, u32[]{:S(2)}) collective-permute-start(bf16[2,144,432]{2,1,0:T(8,128)(2,1)} %dynamic-slice_bitcast_fusion.5), channel_id=1, source_target_pairs={{0,16},{4,20},{8,24},{12,28},{16,0},{20,4},{24,8},{28,12},{1,17},{... | collective-permute-start | bytes 746504 | tf_op jit(solution)/shard_map/ppermute | solution.py:905
  (54 other events, 394.5 us)
Sparse Core Ops, SparseCore 0:
  9.9 41.6 all-gather.3
  123.6 57.8 all-gather.5
  206.7 44.3 reduce-scatter.1
